TPU v7x, 32 devices: a whole 2x2x4 slice. The times are simulated.
32 devices in a mesh: ctx: 8 (over z, core), head: 4 (over y, x).
Axes of the slice: x: 2, y: 2, z: 4, core: 2. Of those that a mesh axis runs over, the one named last changes fastest.
Arguments:
- queries: bfloat16 [512, 16384], P('ctx', 'head'), may hold values from -8000 to 8000
- key_codes: bfloat16 [16384, 1024], P('ctx', 'head'), may hold values from -127 to 127
- value_codes: bfloat16 [16384, 1024], P('ctx', 'head'), may hold values from -127 to 127
- key_scales: int32 [256, 8], P('ctx', 'head'), may hold values from 1 to 16
- value_scales: int32 [256, 8], P('ctx', 'head'), may hold values from 1 to 16
- positions: int32 [512], replicated, may hold values from 0 to 16383
- out_weight: bfloat16 [16384, 16384], P('head', 'ctx'), may hold values from -0.046875 to 0.046875
Outputs:
- projected: bfloat16 [512, 16384], P('head', 'ctx')
All inputs are finite; a program needn't handle non-finite values.
Results may differ from a plain program's by a relative error of at most 0.009.
Values may be sent and summed in bfloat16 or wider, within the bound.
A program may use at most 128 MiB of HBM per device.

v0:
```python
import math

import jax
import jax.numpy as jnp
from jax import lax
from jax.sharding import PartitionSpec as P

HD = 128
BLOCK = 64


QUANT_STEP = 1.0 / 2048.0
MASKED = -1e30


def shifted(value, axis, steps):
    count = lax.axis_size(axis)
    pairs = [(source, (source + steps) % count) for source in range(count)]
    return lax.ppermute(value, axis, pairs)


def hadamard_signs(size_value):
    indices = jnp.arange(size_value, dtype=jnp.int32)
    common = jnp.bitwise_and(indices[:, None], indices[None, :])
    parity = jnp.zeros((size_value, size_value), jnp.int32)
    for shift_bit in range(max(int(size_value).bit_length(), 1)):
        parity = jnp.bitwise_xor(parity, jnp.bitwise_and(jnp.right_shift(common, shift_bit), 1))
    return 1.0 - 2.0 * parity.astype(jnp.float32)


def combine_partials(first, second):
    top_first, total_first, numer_first = first
    top_second, total_second, numer_second = second
    new_top = jnp.maximum(top_first, top_second)
    fade_first = jnp.exp(top_first - new_top)
    fade_second = jnp.exp(top_second - new_top)
    new_total = total_first * fade_first + total_second * fade_second
    new_numer = numer_first * fade_first[..., None] + numer_second * fade_second[..., None]
    return (new_top, new_total, new_numer)


def on_device(queries, key_codes, value_codes, key_scales, value_scales, positions, out_weight):
    q_rows = queries.shape[0]
    kv_local = key_scales.shape[1]
    ctx_local = key_codes.shape[0]
    heads_local = queries.shape[1] // HD
    group_size = heads_local // kv_local
    signs = hadamard_signs(HD).astype(jnp.bfloat16)
    rotated = jnp.einsum(
        "rhd,de->rhe",
        queries.reshape(q_rows, heads_local, HD),
        signs,
        preferred_element_type=jnp.float32,
    )
    rotated = (rotated / math.sqrt(HD)).reshape(q_rows, kv_local, group_size, HD)
    cycle_index = lax.axis_index("ctx")
    cycle_size = lax.axis_size("ctx")
    key_first = cycle_index * ctx_local
    key_factor = (
        jnp.repeat(key_scales.astype(jnp.float32), BLOCK, axis=0) * (QUANT_STEP / math.sqrt(HD))
    ).T
    value_factor = (jnp.repeat(value_scales.astype(jnp.float32), BLOCK, axis=0) * QUANT_STEP).T
    key_heads = key_codes.reshape(ctx_local, kv_local, HD).astype(jnp.float32)
    value_heads = value_codes.reshape(ctx_local, kv_local, HD)
    key_pos = key_first + jnp.arange(ctx_local, dtype=jnp.int32)

    def local_partial(query_block, query_pos):
        scores = jnp.einsum(
            "rgjd,cgd->rgjc",
            query_block,
            key_heads,
            preferred_element_type=jnp.float32,
            precision=lax.Precision.HIGHEST,
        )
        scores = scores * key_factor[None, :, None, :]
        visible = (key_pos[None, :] <= query_pos[:, None])[:, None, None, :]
        scores = jnp.where(visible, scores, MASKED)
        highest = jnp.max(scores, axis=3)
        probs = jnp.where(visible, jnp.exp(scores - highest[..., None]), 0.0)
        row_total = jnp.sum(probs, axis=3)
        weights = (probs * value_factor[None, :, None, :]).astype(jnp.bfloat16)
        numerator = jnp.einsum(
            "rgjc,cgd->rgjd", weights, value_heads, preferred_element_type=jnp.float32
        )
        return (highest, row_total, numerator)

    empty_state = (
        jnp.full((q_rows, kv_local, group_size), MASKED, jnp.float32),
        jnp.zeros((q_rows, kv_local, group_size), jnp.float32),
        jnp.zeros((q_rows, kv_local, group_size, HD), jnp.float32),
    )

    def visit(hop_step, loop_carry):
        query_block, partial_state = loop_carry
        source = (cycle_index - hop_step) % cycle_size
        query_pos = lax.dynamic_slice_in_dim(positions, source * q_rows, q_rows)
        partial_state = combine_partials(partial_state, local_partial(query_block, query_pos))
        query_block = shifted(query_block, "ctx", 1)
        partial_state = shifted((partial_state[0], partial_state[1], partial_state[2]), "ctx", 1)
        return (query_block, partial_state)

    query_block, partial_state = lax.fori_loop(0, cycle_size - 1, visit, (rotated, empty_state))
    source = (cycle_index - (cycle_size - 1)) % cycle_size
    query_pos = lax.dynamic_slice_in_dim(positions, source * q_rows, q_rows)
    partial_state = combine_partials(partial_state, local_partial(query_block, query_pos))
    partial_state = shifted((partial_state[0], partial_state[1], partial_state[2]), "ctx", 1)
    highest, row_total, numerator = partial_state
    normalized = (numerator / row_total[..., None]).astype(jnp.bfloat16)
    restored = jnp.einsum("rgjd,de->rgje", normalized, signs, preferred_element_type=jnp.float32)
    restored = (restored / math.sqrt(HD)).astype(jnp.bfloat16)
    attention = restored.reshape(normalized.shape[0], heads_local * HD)
    attention_rows = lax.all_gather(attention, "ctx", axis=0, tiled=True)
    projected = lax.psum_scatter(
        jnp.dot(attention_rows, out_weight, preferred_element_type=jnp.float32),
        "head",
        scatter_dimension=0,
        tiled=True,
    )
    return projected.astype(jnp.bfloat16)


def solution(mesh):
    in_specs = (
        P("ctx", "head"),
        P("ctx", "head"),
        P("ctx", "head"),
        P("ctx", "head"),
        P("ctx", "head"),
        P(),
        P("head", "ctx"),
    )
    out_specs = P("head", "ctx")
    return jax.shard_map(
        on_device, mesh=mesh, in_specs=in_specs, out_specs=out_specs, check_vma=False
    )
```

profile of v0, /device:TPU:9, one launch (start us, length us, event | category | flops | bytes accessed | tf_op | source)
XLA Modules:
  0.0 592.4 jit_solution(13786696399469174665)
XLA Ops:
  6.5 2.3 copy.47
  10.4 2.3 copy.48
  19.1 389.4 %while.22 = (s32[]{:T(128)}, f32[64,2,16,128]{3,0,2,1:T(8,128)}, f32[64,2,16]{0,2,1:T(8,128)S(1)}, f32[64,2,16]{0,2,1:T(8,128)S(1)}, f32[64,2,16,128]{3,0,2,1:T(...) while((s32[]{:T(128)}, f32[64,2,16,128]{3,0,2,1:T(8,128)}, ...), condition=%wide.region_3.4_spmd.clone, body=%wide.region_0.3_spmd.clone.sunk | while | flops 7575840768 | bytes 72189712 | solution.py:102
  21.6 14.9 %fusion.75 = (f32[64,2,16]{0,2,1:T(8,128)S(1)}, f32[2,2048,64,16]{1,2,3,0:T(8,128)S(1)}) fusion(f32[2,2048]{1,0:T(2,128)S(1)} %bitcast.127, pred[64,2048]{1,0:T(8,128)(4,1)S(1)} %broadcast_compare_fusion.3, f32[64,2,16,128]{3,0,2,1:T(8,128)S(1)} %copy.94, f32[2048,2,128]{2,0,1:T(8,128)S(1)} %get-tuple-element.531), kind=kOutput, calls=%fused_computation.6.clone.1 | convolution fusion | flops 6455031808 | bytes 20078592 | tf_op jit(solution)/shard_map/while/body/eval_jaxpr/rgjd,cgd->rgjc/dot_general | solution.py:68
  36.5 5.4 fusion.76
  42.0 6.8 %fusion.77 = f32[64,2,16,128]{3,0,2,1:T(8,128)} fusion(f32[2,2048,64,16]{1,2,3,0:T(8,128)S(1)} %get-tuple-element.482, f32[2,2048]{1,0:T(2,128)S(1)} %bitcast.136, f32[64,2,16]{0,2,1:T(8,128)S(1)} %get-tuple-element.483, f32[2,2048]{1,0:T(2,128)S(1)} %bitcast.129, pred[64,2048]{1,0:T(8,128)(4,1)S(1)} %broadcast_compare_fusion.3, ...), kind=kOutput, calls=%fused_computation.14.clone.1 | convolution fusion | flops 1099694080 | bytes 20111360 | tf_op jit(solution)/shard_map/while/body/eval_jaxpr/rgjc,cgd->rgjd/dot_general | solution.py:82
  52.4 21.6 %collective-permute-done.1 = f32[64,2,16]{0,2,1:T(8,128)S(1)} collective-permute-done((f32[64,2,16]{0,2,1:T(8,128)S(1)}, f32[64,2,16]{0,2,1:T(8,128)S(1)}, u32[]{:S(2)}, u32[]{:S(2)}) %collective-permute-start.1) | collective-permute-done | bytes 8224 | tf_op jit(solution)/shard_map/while/body/eval_jaxpr/ppermute | solution.py:19
  76.7 14.9 %fusion.75 = (f32[64,2,16]{0,2,1:T(8,128)S(1)}, f32[2,2048,64,16]{1,2,3,0:T(8,128)S(1)}) fusion(f32[2,2048]{1,0:T(2,128)S(1)} %bitcast.127, pred[64,2048]{1,0:T(8,128)(4,1)S(1)} %broadcast_compare_fusion.3, f32[64,2,16,128]{3,0,2,1:T(8,128)S(1)} %copy.94, f32[2048,2,128]{2,0,1:T(8,128)S(1)} %get-tuple-element.531), kind=kOutput, calls=%fused_computation.6.clone.1 | convolution fusion | flops 6455031808 | bytes 20078592 | tf_op jit(solution)/shard_map/while/body/eval_jaxpr/rgjd,cgd->rgjc/dot_general | solution.py:68
  91.6 5.4 fusion.76
  97.1 6.8 %fusion.77 = f32[64,2,16,128]{3,0,2,1:T(8,128)} fusion(f32[2,2048,64,16]{1,2,3,0:T(8,128)S(1)} %get-tuple-element.482, f32[2,2048]{1,0:T(2,128)S(1)} %bitcast.136, f32[64,2,16]{0,2,1:T(8,128)S(1)} %get-tuple-element.483, f32[2,2048]{1,0:T(2,128)S(1)} %bitcast.129, pred[64,2048]{1,0:T(8,128)(4,1)S(1)} %broadcast_compare_fusion.3, ...), kind=kOutput, calls=%fused_computation.14.clone.1 | convolution fusion | flops 1099694080 | bytes 20111360 | tf_op jit(solution)/shard_map/while/body/eval_jaxpr/rgjc,cgd->rgjd/dot_general | solution.py:82
  103.9 2.5 collective-permute-start.3
  108.1 21.6 %collective-permute-done.1 = f32[64,2,16]{0,2,1:T(8,128)S(1)} collective-permute-done((f32[64,2,16]{0,2,1:T(8,128)S(1)}, f32[64,2,16]{0,2,1:T(8,128)S(1)}, u32[]{:S(2)}, u32[]{:S(2)}) %collective-permute-start.1) | collective-permute-done | bytes 8224 | tf_op jit(solution)/shard_map/while/body/eval_jaxpr/ppermute | solution.py:19
  132.4 14.9 %fusion.75 = (f32[64,2,16]{0,2,1:T(8,128)S(1)}, f32[2,2048,64,16]{1,2,3,0:T(8,128)S(1)}) fusion(f32[2,2048]{1,0:T(2,128)S(1)} %bitcast.127, pred[64,2048]{1,0:T(8,128)(4,1)S(1)} %broadcast_compare_fusion.3, f32[64,2,16,128]{3,0,2,1:T(8,128)S(1)} %copy.94, f32[2048,2,128]{2,0,1:T(8,128)S(1)} %get-tuple-element.531), kind=kOutput, calls=%fused_computation.6.clone.1 | convolution fusion | flops 6455031808 | bytes 20078592 | tf_op jit(solution)/shard_map/while/body/eval_jaxpr/rgjd,cgd->rgjc/dot_general | solution.py:68
  147.3 5.4 fusion.76
  152.8 6.8 %fusion.77 = f32[64,2,16,128]{3,0,2,1:T(8,128)} fusion(f32[2,2048,64,16]{1,2,3,0:T(8,128)S(1)} %get-tuple-element.482, f32[2,2048]{1,0:T(2,128)S(1)} %bitcast.136, f32[64,2,16]{0,2,1:T(8,128)S(1)} %get-tuple-element.483, f32[2,2048]{1,0:T(2,128)S(1)} %bitcast.129, pred[64,2048]{1,0:T(8,128)(4,1)S(1)} %broadcast_compare_fusion.3, ...), kind=kOutput, calls=%fused_computation.14.clone.1 | convolution fusion | flops 1099694080 | bytes 20111360 | tf_op jit(solution)/shard_map/while/body/eval_jaxpr/rgjc,cgd->rgjd/dot_general | solution.py:82
  159.6 2.5 collective-permute-start.3
  163.8 21.6 %collective-permute-done.1 = f32[64,2,16]{0,2,1:T(8,128)S(1)} collective-permute-done((f32[64,2,16]{0,2,1:T(8,128)S(1)}, f32[64,2,16]{0,2,1:T(8,128)S(1)}, u32[]{:S(2)}, u32[]{:S(2)}) %collective-permute-start.1) | collective-permute-done | bytes 8224 | tf_op jit(solution)/shard_map/while/body/eval_jaxpr/ppermute | solution.py:19
  188.1 14.9 %fusion.75 = (f32[64,2,16]{0,2,1:T(8,128)S(1)}, f32[2,2048,64,16]{1,2,3,0:T(8,128)S(1)}) fusion(f32[2,2048]{1,0:T(2,128)S(1)} %bitcast.127, pred[64,2048]{1,0:T(8,128)(4,1)S(1)} %broadcast_compare_fusion.3, f32[64,2,16,128]{3,0,2,1:T(8,128)S(1)} %copy.94, f32[2048,2,128]{2,0,1:T(8,128)S(1)} %get-tuple-element.531), kind=kOutput, calls=%fused_computation.6.clone.1 | convolution fusion | flops 6455031808 | bytes 20078592 | tf_op jit(solution)/shard_map/while/body/eval_jaxpr/rgjd,cgd->rgjc/dot_general | solution.py:68
  203.1 5.4 fusion.76
  208.5 6.8 %fusion.77 = f32[64,2,16,128]{3,0,2,1:T(8,128)} fusion(f32[2,2048,64,16]{1,2,3,0:T(8,128)S(1)} %get-tuple-element.482, f32[2,2048]{1,0:T(2,128)S(1)} %bitcast.136, f32[64,2,16]{0,2,1:T(8,128)S(1)} %get-tuple-element.483, f32[2,2048]{1,0:T(2,128)S(1)} %bitcast.129, pred[64,2048]{1,0:T(8,128)(4,1)S(1)} %broadcast_compare_fusion.3, ...), kind=kOutput, calls=%fused_computation.14.clone.1 | convolution fusion | flops 1099694080 | bytes 20111360 | tf_op jit(solution)/shard_map/while/body/eval_jaxpr/rgjc,cgd->rgjd/dot_general | solution.py:82
  215.3 2.5 collective-permute-start.3
  220.4 20.7 %collective-permute-done.1 = f32[64,2,16]{0,2,1:T(8,128)S(1)} collective-permute-done((f32[64,2,16]{0,2,1:T(8,128)S(1)}, f32[64,2,16]{0,2,1:T(8,128)S(1)}, u32[]{:S(2)}, u32[]{:S(2)}) %collective-permute-start.1) | collective-permute-done | bytes 8224 | tf_op jit(solution)/shard_map/while/body/eval_jaxpr/ppermute | solution.py:19
  243.8 14.9 %fusion.75 = (f32[64,2,16]{0,2,1:T(8,128)S(1)}, f32[2,2048,64,16]{1,2,3,0:T(8,128)S(1)}) fusion(f32[2,2048]{1,0:T(2,128)S(1)} %bitcast.127, pred[64,2048]{1,0:T(8,128)(4,1)S(1)} %broadcast_compare_fusion.3, f32[64,2,16,128]{3,0,2,1:T(8,128)S(1)} %copy.94, f32[2048,2,128]{2,0,1:T(8,128)S(1)} %get-tuple-element.531), kind=kOutput, calls=%fused_computation.6.clone.1 | convolution fusion | flops 6455031808 | bytes 20078592 | tf_op jit(solution)/shard_map/while/body/eval_jaxpr/rgjd,cgd->rgjc/dot_general | solution.py:68
  258.8 5.4 fusion.76
  264.2 6.8 %fusion.77 = f32[64,2,16,128]{3,0,2,1:T(8,128)} fusion(f32[2,2048,64,16]{1,2,3,0:T(8,128)S(1)} %get-tuple-element.482, f32[2,2048]{1,0:T(2,128)S(1)} %bitcast.136, f32[64,2,16]{0,2,1:T(8,128)S(1)} %get-tuple-element.483, f32[2,2048]{1,0:T(2,128)S(1)} %bitcast.129, pred[64,2048]{1,0:T(8,128)(4,1)S(1)} %broadcast_compare_fusion.3, ...), kind=kOutput, calls=%fused_computation.14.clone.1 | convolution fusion | flops 1099694080 | bytes 20111360 | tf_op jit(solution)/shard_map/while/body/eval_jaxpr/rgjc,cgd->rgjd/dot_general | solution.py:82
  271.0 2.5 collective-permute-start.3
  275.2 2.7 collective-permute-start.2
  277.9 18.9 %collective-permute-done.1 = f32[64,2,16]{0,2,1:T(8,128)S(1)} collective-permute-done((f32[64,2,16]{0,2,1:T(8,128)S(1)}, f32[64,2,16]{0,2,1:T(8,128)S(1)}, u32[]{:S(2)}, u32[]{:S(2)}) %collective-permute-start.1) | collective-permute-done | bytes 8224 | tf_op jit(solution)/shard_map/while/body/eval_jaxpr/ppermute | solution.py:19
  299.5 14.9 %fusion.75 = (f32[64,2,16]{0,2,1:T(8,128)S(1)}, f32[2,2048,64,16]{1,2,3,0:T(8,128)S(1)}) fusion(f32[2,2048]{1,0:T(2,128)S(1)} %bitcast.127, pred[64,2048]{1,0:T(8,128)(4,1)S(1)} %broadcast_compare_fusion.3, f32[64,2,16,128]{3,0,2,1:T(8,128)S(1)} %copy.94, f32[2048,2,128]{2,0,1:T(8,128)S(1)} %get-tuple-element.531), kind=kOutput, calls=%fused_computation.6.clone.1 | convolution fusion | flops 6455031808 | bytes 20078592 | tf_op jit(solution)/shard_map/while/body/eval_jaxpr/rgjd,cgd->rgjc/dot_general | solution.py:68
  314.5 5.4 fusion.76
  319.9 6.8 %fusion.77 = f32[64,2,16,128]{3,0,2,1:T(8,128)} fusion(f32[2,2048,64,16]{1,2,3,0:T(8,128)S(1)} %get-tuple-element.482, f32[2,2048]{1,0:T(2,128)S(1)} %bitcast.136, f32[64,2,16]{0,2,1:T(8,128)S(1)} %get-tuple-element.483, f32[2,2048]{1,0:T(2,128)S(1)} %bitcast.129, pred[64,2048]{1,0:T(8,128)(4,1)S(1)} %broadcast_compare_fusion.3, ...), kind=kOutput, calls=%fused_computation.14.clone.1 | convolution fusion | flops 1099694080 | bytes 20111360 | tf_op jit(solution)/shard_map/while/body/eval_jaxpr/rgjc,cgd->rgjd/dot_general | solution.py:82
  326.7 2.5 collective-permute-start.3
  330.9 4.5 collective-permute-start.2
  335.4 17.1 %collective-permute-done.1 = f32[64,2,16]{0,2,1:T(8,128)S(1)} collective-permute-done((f32[64,2,16]{0,2,1:T(8,128)S(1)}, f32[64,2,16]{0,2,1:T(8,128)S(1)}, u32[]{:S(2)}, u32[]{:S(2)}) %collective-permute-start.1) | collective-permute-done | bytes 8224 | tf_op jit(solution)/shard_map/while/body/eval_jaxpr/ppermute | solution.py:19
  355.2 14.9 %fusion.75 = (f32[64,2,16]{0,2,1:T(8,128)S(1)}, f32[2,2048,64,16]{1,2,3,0:T(8,128)S(1)}) fusion(f32[2,2048]{1,0:T(2,128)S(1)} %bitcast.127, pred[64,2048]{1,0:T(8,128)(4,1)S(1)} %broadcast_compare_fusion.3, f32[64,2,16,128]{3,0,2,1:T(8,128)S(1)} %copy.94, f32[2048,2,128]{2,0,1:T(8,128)S(1)} %get-tuple-element.531), kind=kOutput, calls=%fused_computation.6.clone.1 | convolution fusion | flops 6455031808 | bytes 20078592 | tf_op jit(solution)/shard_map/while/body/eval_jaxpr/rgjd,cgd->rgjc/dot_general | solution.py:68
  370.2 5.4 fusion.76
  375.6 6.8 %fusion.77 = f32[64,2,16,128]{3,0,2,1:T(8,128)} fusion(f32[2,2048,64,16]{1,2,3,0:T(8,128)S(1)} %get-tuple-element.482, f32[2,2048]{1,0:T(2,128)S(1)} %bitcast.136, f32[64,2,16]{0,2,1:T(8,128)S(1)} %get-tuple-element.483, f32[2,2048]{1,0:T(2,128)S(1)} %bitcast.129, pred[64,2048]{1,0:T(8,128)(4,1)S(1)} %broadcast_compare_fusion.3, ...), kind=kOutput, calls=%fused_computation.14.clone.1 | convolution fusion | flops 1099694080 | bytes 20111360 | tf_op jit(solution)/shard_map/while/body/eval_jaxpr/rgjc,cgd->rgjd/dot_general | solution.py:82
  382.5 2.5 collective-permute-start.3
  386.6 6.3 %collective-permute-start.2 = (f32[64,2,16]{0,2,1:T(8,128)S(1)}, f32[64,2,16]{0,2,1:T(8,128)S(1)}, u32[]{:S(2)}, u32[]{:S(2)}) collective-permute-start(f32[64,2,16]{0,2,1:T(8,128)S(1)} %get-tuple-element.485), channel_id=1, source_target_pairs={{0,4},{4,8},{8,12},{12,16},{16,20},{20,24},{24,28},{28,0},{1,5},{5... | collective-permute-start | bytes 24584 | tf_op jit(solution)/shard_map/while/body/eval_jaxpr/ppermute | solution.py:19
  392.9 15.3 %collective-permute-done.1 = f32[64,2,16]{0,2,1:T(8,128)S(1)} collective-permute-done((f32[64,2,16]{0,2,1:T(8,128)S(1)}, f32[64,2,16]{0,2,1:T(8,128)S(1)}, u32[]{:S(2)}, u32[]{:S(2)}) %collective-permute-start.1) | collective-permute-done | bytes 8224 | tf_op jit(solution)/shard_map/while/body/eval_jaxpr/ppermute | solution.py:19
  408.5 13.8 %bitcast_reduce_fusion = (f32[64,2,16]{2,0,1:T(8,128)S(1)}, f32[2,64,16,2048]{3,2,1,0:T(8,128)}) fusion(f32[2,2048]{1,0:T(2,128)S(1)} %bitcast.137, pred[64,2048]{1,0:T(8,128)(4,1)S(1)} %broadcast_compare_fusion.1, bf16[2048,2,128,1]{0,2,3,1:T(8,128)(2,1)} %bitcast.131, f32[64,2,16,128]{3,0,2,1:T(8,128)} %get-tuple-element.297), kind=kOutput, calls=%fused_computation.24 | convolution fusion | flops 6455031808 | bytes 19030016 | tf_op jit(solution)/shard_map/rgjd,cgd->rgjc/dot_general | solution.py:68
  422.4 8.7 %fusion.20 = f32[64,2,16]{2,0,1:T(8,128)S(1)} fusion(f32[2,64,16,2048]{3,2,1,0:T(8,128)} %get-tuple-element.400, f32[64,2,16]{2,0,1:T(8,128)S(1)} %get-tuple-element.399, f32[2,2048]{1,0:T(2,128)S(1)} %bitcast.138, pred[64,2048]{1,0:T(8,128)(4,1)S(1)} %broadcast_compare_fusion.1), kind=kLoop, calls=%fused_computation.29 | loop fusion | flops 20969472 | bytes 16941056 | tf_op jit(solution)/shard_map/reduce_sum | solution.py:80
  431.5 8.9 %fusion.26 = f32[64,2,16,128]{3,2,0,1:T(8,128)S(1)} fusion(bf16[2048,2,128,1]{0,2,3,1:T(8,128)(2,1)S(1)} %bitcast.133, f32[2,64,16,2048]{3,2,1,0:T(8,128)} %get-tuple-element.400, f32[2,2048]{1,0:T(2,128)S(1)} %bitcast.140, f32[64,2,16]{2,0,1:T(8,128)S(1)} %get-tuple-element.399, f32[2,2048]{1,0:T(2,128)S(1)} %bitcast.139, ...), kind=kOutput, calls=%fused_computation.37 | convolution fusion | flops 1099694080 | bytes 20111360 | tf_op jit(solution)/shard_map/rgjc,cgd->rgjd/dot_general | solution.py:82
  440.4 2.6 collective-permute-start.4
  443.0 11.9 %collective-permute-done.5 = f32[64,2,16]{0,2,1:T(8,128)S(1)} collective-permute-done((f32[64,2,16]{0,2,1:T(8,128)S(1)}, f32[64,2,16]{0,2,1:T(8,128)S(1)}, u32[]{:S(2)}, u32[]{:S(2)}) %collective-permute-start.5) | collective-permute-done | bytes 8224 | tf_op jit(solution)/shard_map/ppermute | solution.py:19
  456.5 59.2 %all-gather.2.cloned.1.call-done = bf16[512,4096]{1,0:T(8,128)(2,1)} async-done(((bf16[64,4096]{1,0:T(8,128)(2,1)}), bf16[512,4096]{1,0:T(8,128)(2,1)}) %all-gather.2.cloned.1.call-update) | async-done | bytes 4194320 | tf_op jit(solution)/shard_map/all_gather | solution.py:112
  515.7 15.0 %fusion.61 = f32[512,2048]{1,0:T(8,128)} fusion(bf16[512,4096]{1,0:T(8,128)(2,1)} %all-gather.2.cloned.1.call-done, bf16[4096,2048]{1,0:T(8,128)(2,1)} %param.15), kind=kOutput, calls=%fused_computation.81 | convolution fusion | flops 8589934592 | bytes 25165824 | tf_op jit(solution)/shard_map/dot_general | solution.py:114
  530.7 52.7 %reduce-scatter.2.cloned.1.call-done = f32[128,2048]{1,0:T(8,128)} async-done(((f32[512,2048]{1,0:T(8,128)}), f32[128,2048]{1,0:T(8,128)}) %reduce-scatter.2.cloned.1.call-update) | async-done | bytes 1048592 | tf_op jit(solution)/shard_map/reduce_scatter | solution.py:113
  (152 shorter events, 45.6 us)
Async XLA Ops:
  6.5 8.3 %copy-start = (bf16[64,4096]{1,0:T(8,128)(2,1)S(1)}, bf16[64,4096]{1,0:T(8,128)(2,1)}, u32[]{:S(2)}) copy-start(bf16[64,4096]{1,0:T(8,128)(2,1)} %param.9) | copy-start | bytes 1572868
  6.5 509.2 %all-gather.2.cloned.1.call-start = ((), (), s32[]{:S(2)}) async-start(), calls=%async_computation.1 | async-start | bytes 4718592 | tf_op jit(solution)/shard_map/all_gather | solution.py:112
  21.6 20.4 %copy-start.3 = (bf16[2048,2,128]{2,0,1:T(8,128)(2,1)S(1)}, bf16[2048,2,128]{2,0,1:T(8,128)(2,1)}, u32[]{:S(2)}) copy-start(bf16[2048,2,128]{2,0,1:T(8,128)(2,1)} %get-tuple-element.532) | copy-start | bytes 3145732 | tf_op jit(solution)/shard_map/while
  48.8 25.4 %collective-permute-start.3 = (f32[64,2,16,128]{3,0,2,1:T(8,128)}, f32[64,2,16,128]{3,0,2,1:T(8,128)}, u32[]{:S(2)}, u32[]{:S(2)}) collective-permute-start(f32[64,2,16,128]{3,0,2,1:T(8,128)} %fusion.77), channel_id=1, source_target_pairs={{0,4},{4,8},{8,12},{12,16},{16,20},{20,24},{24,28},{28,0},{1,5},{5... | collective-permute-start | bytes 3145736 | tf_op jit(solution)/shard_map/while/body/eval_jaxpr/ppermute | solution.py:19
  50.6 23.5 %collective-permute-start = (f32[64,2,16,128]{3,0,2,1:T(8,128)S(1)}, f32[64,2,16,128]{3,0,2,1:T(8,128)}, u32[]{:S(2)}, u32[]{:S(2)}) collective-permute-start(f32[64,2,16,128]{3,0,2,1:T(8,128)S(1)} %copy.94), channel_id=1, source_target_pairs={{0,4},{4,8},{8,12},{12,16},{16,20},{20,24},{24,28},{28,0},{1,5},{5... | collective-permute-start | bytes 3145736 | tf_op jit(solution)/shard_map/while/body/eval_jaxpr/ppermute | solution.py:19
  50.7 23.3 %collective-permute-start.1 = (f32[64,2,16]{0,2,1:T(8,128)S(1)}, f32[64,2,16]{0,2,1:T(8,128)S(1)}, u32[]{:S(2)}, u32[]{:S(2)}) collective-permute-start(f32[64,2,16]{0,2,1:T(8,128)S(1)} %get-tuple-element.484), channel_id=1, source_target_pairs={{0,4},{4,8},{8,12},{12,16},{16,20},{20,24},{24,28},{28,0},{1,5},{5... | collective-permute-start | bytes 24584 | tf_op jit(solution)/shard_map/while/body/eval_jaxpr/ppermute | solution.py:19
  52.3 21.8 %collective-permute-start.2 = (f32[64,2,16]{0,2,1:T(8,128)S(1)}, f32[64,2,16]{0,2,1:T(8,128)S(1)}, u32[]{:S(2)}, u32[]{:S(2)}) collective-permute-start(f32[64,2,16]{0,2,1:T(8,128)S(1)} %get-tuple-element.485), channel_id=1, source_target_pairs={{0,4},{4,8},{8,12},{12,16},{16,20},{20,24},{24,28},{28,0},{1,5},{5... | collective-permute-start | bytes 24584 | tf_op jit(solution)/shard_map/while/body/eval_jaxpr/ppermute | solution.py:19
  76.7 20.4 %copy-start.3 = (bf16[2048,2,128]{2,0,1:T(8,128)(2,1)S(1)}, bf16[2048,2,128]{2,0,1:T(8,128)(2,1)}, u32[]{:S(2)}) copy-start(bf16[2048,2,128]{2,0,1:T(8,128)(2,1)} %get-tuple-element.532) | copy-start | bytes 3145732 | tf_op jit(solution)/shard_map/while
  103.9 26.0 %collective-permute-start.3 = (f32[64,2,16,128]{3,0,2,1:T(8,128)}, f32[64,2,16,128]{3,0,2,1:T(8,128)}, u32[]{:S(2)}, u32[]{:S(2)}) collective-permute-start(f32[64,2,16,128]{3,0,2,1:T(8,128)} %fusion.77), channel_id=1, source_target_pairs={{0,4},{4,8},{8,12},{12,16},{16,20},{20,24},{24,28},{28,0},{1,5},{5... | collective-permute-start | bytes 3145736 | tf_op jit(solution)/shard_map/while/body/eval_jaxpr/ppermute | solution.py:19
  106.4 23.5 %collective-permute-start = (f32[64,2,16,128]{3,0,2,1:T(8,128)S(1)}, f32[64,2,16,128]{3,0,2,1:T(8,128)}, u32[]{:S(2)}, u32[]{:S(2)}) collective-permute-start(f32[64,2,16,128]{3,0,2,1:T(8,128)S(1)} %copy.94), channel_id=1, source_target_pairs={{0,4},{4,8},{8,12},{12,16},{16,20},{20,24},{24,28},{28,0},{1,5},{5... | collective-permute-start | bytes 3145736 | tf_op jit(solution)/shard_map/while/body/eval_jaxpr/ppermute | solution.py:19
  106.4 23.3 %collective-permute-start.1 = (f32[64,2,16]{0,2,1:T(8,128)S(1)}, f32[64,2,16]{0,2,1:T(8,128)S(1)}, u32[]{:S(2)}, u32[]{:S(2)}) collective-permute-start(f32[64,2,16]{0,2,1:T(8,128)S(1)} %get-tuple-element.484), channel_id=1, source_target_pairs={{0,4},{4,8},{8,12},{12,16},{16,20},{20,24},{24,28},{28,0},{1,5},{5... | collective-permute-start | bytes 24584 | tf_op jit(solution)/shard_map/while/body/eval_jaxpr/ppermute | solution.py:19
  108.1 21.8 %collective-permute-start.2 = (f32[64,2,16]{0,2,1:T(8,128)S(1)}, f32[64,2,16]{0,2,1:T(8,128)S(1)}, u32[]{:S(2)}, u32[]{:S(2)}) collective-permute-start(f32[64,2,16]{0,2,1:T(8,128)S(1)} %get-tuple-element.485), channel_id=1, source_target_pairs={{0,4},{4,8},{8,12},{12,16},{16,20},{20,24},{24,28},{28,0},{1,5},{5... | collective-permute-start | bytes 24584 | tf_op jit(solution)/shard_map/while/body/eval_jaxpr/ppermute | solution.py:19
  132.4 20.4 %copy-start.3 = (bf16[2048,2,128]{2,0,1:T(8,128)(2,1)S(1)}, bf16[2048,2,128]{2,0,1:T(8,128)(2,1)}, u32[]{:S(2)}) copy-start(bf16[2048,2,128]{2,0,1:T(8,128)(2,1)} %get-tuple-element.532) | copy-start | bytes 3145732 | tf_op jit(solution)/shard_map/while
  159.6 26.0 %collective-permute-start.3 = (f32[64,2,16,128]{3,0,2,1:T(8,128)}, f32[64,2,16,128]{3,0,2,1:T(8,128)}, u32[]{:S(2)}, u32[]{:S(2)}) collective-permute-start(f32[64,2,16,128]{3,0,2,1:T(8,128)} %fusion.77), channel_id=1, source_target_pairs={{0,4},{4,8},{8,12},{12,16},{16,20},{20,24},{24,28},{28,0},{1,5},{5... | collective-permute-start | bytes 3145736 | tf_op jit(solution)/shard_map/while/body/eval_jaxpr/ppermute | solution.py:19
  162.1 23.5 %collective-permute-start = (f32[64,2,16,128]{3,0,2,1:T(8,128)S(1)}, f32[64,2,16,128]{3,0,2,1:T(8,128)}, u32[]{:S(2)}, u32[]{:S(2)}) collective-permute-start(f32[64,2,16,128]{3,0,2,1:T(8,128)S(1)} %copy.94), channel_id=1, source_target_pairs={{0,4},{4,8},{8,12},{12,16},{16,20},{20,24},{24,28},{28,0},{1,5},{5... | collective-permute-start | bytes 3145736 | tf_op jit(solution)/shard_map/while/body/eval_jaxpr/ppermute | solution.py:19
  162.1 23.3 %collective-permute-start.1 = (f32[64,2,16]{0,2,1:T(8,128)S(1)}, f32[64,2,16]{0,2,1:T(8,128)S(1)}, u32[]{:S(2)}, u32[]{:S(2)}) collective-permute-start(f32[64,2,16]{0,2,1:T(8,128)S(1)} %get-tuple-element.484), channel_id=1, source_target_pairs={{0,4},{4,8},{8,12},{12,16},{16,20},{20,24},{24,28},{28,0},{1,5},{5... | collective-permute-start | bytes 24584 | tf_op jit(solution)/shard_map/while/body/eval_jaxpr/ppermute | solution.py:19
  163.8 21.8 %collective-permute-start.2 = (f32[64,2,16]{0,2,1:T(8,128)S(1)}, f32[64,2,16]{0,2,1:T(8,128)S(1)}, u32[]{:S(2)}, u32[]{:S(2)}) collective-permute-start(f32[64,2,16]{0,2,1:T(8,128)S(1)} %get-tuple-element.485), channel_id=1, source_target_pairs={{0,4},{4,8},{8,12},{12,16},{16,20},{20,24},{24,28},{28,0},{1,5},{5... | collective-permute-start | bytes 24584 | tf_op jit(solution)/shard_map/while/body/eval_jaxpr/ppermute | solution.py:19
  188.1 20.4 %copy-start.3 = (bf16[2048,2,128]{2,0,1:T(8,128)(2,1)S(1)}, bf16[2048,2,128]{2,0,1:T(8,128)(2,1)}, u32[]{:S(2)}) copy-start(bf16[2048,2,128]{2,0,1:T(8,128)(2,1)} %get-tuple-element.532) | copy-start | bytes 3145732 | tf_op jit(solution)/shard_map/while
  215.3 26.0 %collective-permute-start.3 = (f32[64,2,16,128]{3,0,2,1:T(8,128)}, f32[64,2,16,128]{3,0,2,1:T(8,128)}, u32[]{:S(2)}, u32[]{:S(2)}) collective-permute-start(f32[64,2,16,128]{3,0,2,1:T(8,128)} %fusion.77), channel_id=1, source_target_pairs={{0,4},{4,8},{8,12},{12,16},{16,20},{20,24},{24,28},{28,0},{1,5},{5... | collective-permute-start | bytes 3145736 | tf_op jit(solution)/shard_map/while/body/eval_jaxpr/ppermute | solution.py:19
  217.8 23.5 %collective-permute-start = (f32[64,2,16,128]{3,0,2,1:T(8,128)S(1)}, f32[64,2,16,128]{3,0,2,1:T(8,128)}, u32[]{:S(2)}, u32[]{:S(2)}) collective-permute-start(f32[64,2,16,128]{3,0,2,1:T(8,128)S(1)} %copy.94), channel_id=1, source_target_pairs={{0,4},{4,8},{8,12},{12,16},{16,20},{20,24},{24,28},{28,0},{1,5},{5... | collective-permute-start | bytes 3145736 | tf_op jit(solution)/shard_map/while/body/eval_jaxpr/ppermute | solution.py:19
  217.8 23.3 %collective-permute-start.1 = (f32[64,2,16]{0,2,1:T(8,128)S(1)}, f32[64,2,16]{0,2,1:T(8,128)S(1)}, u32[]{:S(2)}, u32[]{:S(2)}) collective-permute-start(f32[64,2,16]{0,2,1:T(8,128)S(1)} %get-tuple-element.484), channel_id=1, source_target_pairs={{0,4},{4,8},{8,12},{12,16},{16,20},{20,24},{24,28},{28,0},{1,5},{5... | collective-permute-start | bytes 24584 | tf_op jit(solution)/shard_map/while/body/eval_jaxpr/ppermute | solution.py:19
  219.5 21.8 %collective-permute-start.2 = (f32[64,2,16]{0,2,1:T(8,128)S(1)}, f32[64,2,16]{0,2,1:T(8,128)S(1)}, u32[]{:S(2)}, u32[]{:S(2)}) collective-permute-start(f32[64,2,16]{0,2,1:T(8,128)S(1)} %get-tuple-element.485), channel_id=1, source_target_pairs={{0,4},{4,8},{8,12},{12,16},{16,20},{20,24},{24,28},{28,0},{1,5},{5... | collective-permute-start | bytes 24584 | tf_op jit(solution)/shard_map/while/body/eval_jaxpr/ppermute | solution.py:19
  243.8 20.4 %copy-start.3 = (bf16[2048,2,128]{2,0,1:T(8,128)(2,1)S(1)}, bf16[2048,2,128]{2,0,1:T(8,128)(2,1)}, u32[]{:S(2)}) copy-start(bf16[2048,2,128]{2,0,1:T(8,128)(2,1)} %get-tuple-element.532) | copy-start | bytes 3145732 | tf_op jit(solution)/shard_map/while
  271.0 26.0 %collective-permute-start.3 = (f32[64,2,16,128]{3,0,2,1:T(8,128)}, f32[64,2,16,128]{3,0,2,1:T(8,128)}, u32[]{:S(2)}, u32[]{:S(2)}) collective-permute-start(f32[64,2,16,128]{3,0,2,1:T(8,128)} %fusion.77), channel_id=1, source_target_pairs={{0,4},{4,8},{8,12},{12,16},{16,20},{20,24},{24,28},{28,0},{1,5},{5... | collective-permute-start | bytes 3145736 | tf_op jit(solution)/shard_map/while/body/eval_jaxpr/ppermute | solution.py:19
  273.5 23.5 %collective-permute-start = (f32[64,2,16,128]{3,0,2,1:T(8,128)S(1)}, f32[64,2,16,128]{3,0,2,1:T(8,128)}, u32[]{:S(2)}, u32[]{:S(2)}) collective-permute-start(f32[64,2,16,128]{3,0,2,1:T(8,128)S(1)} %copy.94), channel_id=1, source_target_pairs={{0,4},{4,8},{8,12},{12,16},{16,20},{20,24},{24,28},{28,0},{1,5},{5... | collective-permute-start | bytes 3145736 | tf_op jit(solution)/shard_map/while/body/eval_jaxpr/ppermute | solution.py:19
  273.5 23.3 %collective-permute-start.1 = (f32[64,2,16]{0,2,1:T(8,128)S(1)}, f32[64,2,16]{0,2,1:T(8,128)S(1)}, u32[]{:S(2)}, u32[]{:S(2)}) collective-permute-start(f32[64,2,16]{0,2,1:T(8,128)S(1)} %get-tuple-element.484), channel_id=1, source_target_pairs={{0,4},{4,8},{8,12},{12,16},{16,20},{20,24},{24,28},{28,0},{1,5},{5... | collective-permute-start | bytes 24584 | tf_op jit(solution)/shard_map/while/body/eval_jaxpr/ppermute | solution.py:19
  275.2 21.8 %collective-permute-start.2 = (f32[64,2,16]{0,2,1:T(8,128)S(1)}, f32[64,2,16]{0,2,1:T(8,128)S(1)}, u32[]{:S(2)}, u32[]{:S(2)}) collective-permute-start(f32[64,2,16]{0,2,1:T(8,128)S(1)} %get-tuple-element.485), channel_id=1, source_target_pairs={{0,4},{4,8},{8,12},{12,16},{16,20},{20,24},{24,28},{28,0},{1,5},{5... | collective-permute-start | bytes 24584 | tf_op jit(solution)/shard_map/while/body/eval_jaxpr/ppermute | solution.py:19
  299.5 20.4 %copy-start.3 = (bf16[2048,2,128]{2,0,1:T(8,128)(2,1)S(1)}, bf16[2048,2,128]{2,0,1:T(8,128)(2,1)}, u32[]{:S(2)}) copy-start(bf16[2048,2,128]{2,0,1:T(8,128)(2,1)} %get-tuple-element.532) | copy-start | bytes 3145732 | tf_op jit(solution)/shard_map/while
  326.7 26.0 %collective-permute-start.3 = (f32[64,2,16,128]{3,0,2,1:T(8,128)}, f32[64,2,16,128]{3,0,2,1:T(8,128)}, u32[]{:S(2)}, u32[]{:S(2)}) collective-permute-start(f32[64,2,16,128]{3,0,2,1:T(8,128)} %fusion.77), channel_id=1, source_target_pairs={{0,4},{4,8},{8,12},{12,16},{16,20},{20,24},{24,28},{28,0},{1,5},{5... | collective-permute-start | bytes 3145736 | tf_op jit(solution)/shard_map/while/body/eval_jaxpr/ppermute | solution.py:19
  329.2 23.5 %collective-permute-start = (f32[64,2,16,128]{3,0,2,1:T(8,128)S(1)}, f32[64,2,16,128]{3,0,2,1:T(8,128)}, u32[]{:S(2)}, u32[]{:S(2)}) collective-permute-start(f32[64,2,16,128]{3,0,2,1:T(8,128)S(1)} %copy.94), channel_id=1, source_target_pairs={{0,4},{4,8},{8,12},{12,16},{16,20},{20,24},{24,28},{28,0},{1,5},{5... | collective-permute-start | bytes 3145736 | tf_op jit(solution)/shard_map/while/body/eval_jaxpr/ppermute | solution.py:19
  329.3 23.3 %collective-permute-start.1 = (f32[64,2,16]{0,2,1:T(8,128)S(1)}, f32[64,2,16]{0,2,1:T(8,128)S(1)}, u32[]{:S(2)}, u32[]{:S(2)}) collective-permute-start(f32[64,2,16]{0,2,1:T(8,128)S(1)} %get-tuple-element.484), channel_id=1, source_target_pairs={{0,4},{4,8},{8,12},{12,16},{16,20},{20,24},{24,28},{28,0},{1,5},{5... | collective-permute-start | bytes 24584 | tf_op jit(solution)/shard_map/while/body/eval_jaxpr/ppermute | solution.py:19
  330.9 21.8 %collective-permute-start.2 = (f32[64,2,16]{0,2,1:T(8,128)S(1)}, f32[64,2,16]{0,2,1:T(8,128)S(1)}, u32[]{:S(2)}, u32[]{:S(2)}) collective-permute-start(f32[64,2,16]{0,2,1:T(8,128)S(1)} %get-tuple-element.485), channel_id=1, source_target_pairs={{0,4},{4,8},{8,12},{12,16},{16,20},{20,24},{24,28},{28,0},{1,5},{5... | collective-permute-start | bytes 24584 | tf_op jit(solution)/shard_map/while/body/eval_jaxpr/ppermute | solution.py:19
  355.2 20.4 %copy-start.3 = (bf16[2048,2,128]{2,0,1:T(8,128)(2,1)S(1)}, bf16[2048,2,128]{2,0,1:T(8,128)(2,1)}, u32[]{:S(2)}) copy-start(bf16[2048,2,128]{2,0,1:T(8,128)(2,1)} %get-tuple-element.532) | copy-start | bytes 3145732 | tf_op jit(solution)/shard_map/while
  382.5 26.0 %collective-permute-start.3 = (f32[64,2,16,128]{3,0,2,1:T(8,128)}, f32[64,2,16,128]{3,0,2,1:T(8,128)}, u32[]{:S(2)}, u32[]{:S(2)}) collective-permute-start(f32[64,2,16,128]{3,0,2,1:T(8,128)} %fusion.77), channel_id=1, source_target_pairs={{0,4},{4,8},{8,12},{12,16},{16,20},{20,24},{24,28},{28,0},{1,5},{5... | collective-permute-start | bytes 3145736 | tf_op jit(solution)/shard_map/while/body/eval_jaxpr/ppermute | solution.py:19
  384.9 23.5 %collective-permute-start = (f32[64,2,16,128]{3,0,2,1:T(8,128)S(1)}, f32[64,2,16,128]{3,0,2,1:T(8,128)}, u32[]{:S(2)}, u32[]{:S(2)}) collective-permute-start(f32[64,2,16,128]{3,0,2,1:T(8,128)S(1)} %copy.94), channel_id=1, source_target_pairs={{0,4},{4,8},{8,12},{12,16},{16,20},{20,24},{24,28},{28,0},{1,5},{5... | collective-permute-start | bytes 3145736 | tf_op jit(solution)/shard_map/while/body/eval_jaxpr/ppermute | solution.py:19
  385.0 23.3 %collective-permute-start.1 = (f32[64,2,16]{0,2,1:T(8,128)S(1)}, f32[64,2,16]{0,2,1:T(8,128)S(1)}, u32[]{:S(2)}, u32[]{:S(2)}) collective-permute-start(f32[64,2,16]{0,2,1:T(8,128)S(1)} %get-tuple-element.484), channel_id=1, source_target_pairs={{0,4},{4,8},{8,12},{12,16},{16,20},{20,24},{24,28},{28,0},{1,5},{5... | collective-permute-start | bytes 24584 | tf_op jit(solution)/shard_map/while/body/eval_jaxpr/ppermute | solution.py:19
  386.6 21.8 %collective-permute-start.2 = (f32[64,2,16]{0,2,1:T(8,128)S(1)}, f32[64,2,16]{0,2,1:T(8,128)S(1)}, u32[]{:S(2)}, u32[]{:S(2)}) collective-permute-start(f32[64,2,16]{0,2,1:T(8,128)S(1)} %get-tuple-element.485), channel_id=1, source_target_pairs={{0,4},{4,8},{8,12},{12,16},{16,20},{20,24},{24,28},{28,0},{1,5},{5... | collective-permute-start | bytes 24584 | tf_op jit(solution)/shard_map/while/body/eval_jaxpr/ppermute | solution.py:19
  408.5 23.0 %copy-start.2 = (bf16[2048,256]{0,1:T(8,128)(2,1)S(1)}, bf16[2048,256]{0,1:T(8,128)(2,1)}, u32[]{:S(2)}) copy-start(bf16[2048,256]{0,1:T(8,128)(2,1)} %copy.48) | copy-start | bytes 3145732
  440.4 14.6 %collective-permute-start.4 = (f32[64,2,16,128]{3,2,0,1:T(8,128)S(1)}, f32[64,2,16,128]{3,2,0,1:T(8,128)S(1)}, u32[]{:S(2)}, u32[]{:S(2)}) collective-permute-start(f32[64,2,16,128]{3,2,0,1:T(8,128)S(1)} %fusion.26), channel_id=1, source_target_pairs={{0,4},{4,8},{8,12},{12,16},{16,20},{20,24},{24,28},{28,0},{1,5},{5... | collective-permute-start | bytes 3145736 | tf_op jit(solution)/shard_map/ppermute | solution.py:19
  442.9 11.9 %collective-permute-start.5 = (f32[64,2,16]{0,2,1:T(8,128)S(1)}, f32[64,2,16]{0,2,1:T(8,128)S(1)}, u32[]{:S(2)}, u32[]{:S(2)}) collective-permute-start(f32[64,2,16]{0,2,1:T(8,128)S(1)} %get-tuple-element.394), channel_id=1, source_target_pairs={{0,4},{4,8},{8,12},{12,16},{16,20},{20,24},{24,28},{28,0},{1,5},{5... | collective-permute-start | bytes 24584 | tf_op jit(solution)/shard_map/ppermute | solution.py:19
  456.4 127.0 %reduce-scatter.2.cloned.1.call-start = ((), (), s32[]{:S(2)}) async-start(), calls=%async_computation.2 | async-start | bytes 5242880 | tf_op jit(solution)/shard_map/reduce_scatter | solution.py:113
  515.7 69.8 %copy-start.1 = (bf16[64,4096]{1,0:T(8,128)(2,1)S(1)}, bf16[64,4096]{1,0:T(8,128)(2,1)}, u32[]{:S(2)}) copy-start(bf16[64,4096]{1,0:T(8,128)(2,1)} %param.9) | copy-start | bytes 1572868
Sparse Core Ops, SparseCore 0:
  456.6 59.1 all-gather.1
  530.9 52.5 reduce-scatter.1
where the time goes:
time: 595 us; the launch traced here: 592 us
  waiting for transfers between devices  262 us (44%)
  matrix products  192 us (32%)
  other arithmetic  50.5 us (8%)
  starting transfers between devices  45.9 us (8%)
  local copies, waits for them, and re-layouts  28 us (5%)
  between operations  13.5 us (2%)
    ppermute x30, waiting for transfers between devices, shifted(): return lax.ppermute(value, axis, pairs)  150 us
    dot_general x8, matrix products, local_partial(): jnp.einsum('rgjd,cgd->rgjc', query_block, key_heads, preferred_element_ty...  118 us
    all_gather x1, waiting for transfers between devices, on_device(): attention_rows = lax.all_gather(attention, 'ctx', axis=0, tiled=True)  59.2 us
    dot_general x8, matrix products, local_partial(): jnp.einsum('rgjc,cgd->rgjd', weights, value_heads, preferred_element_type...  56.7 us
    reduce_scatter x1, waiting for transfers between devices, on_device(): lax.psum_scatter(jnp.dot(attention_rows, out_weight, preferred_element_ty...  52.7 us
    reduce_sum x8, other arithmetic, local_partial(): row_total = jnp.sum(probs, axis=3)  46.4 us
    ppermute x30, starting transfers between devices, shifted(): return lax.ppermute(value, axis, pairs)  45.9 us
    dot_general x1, matrix products, on_device(): jnp.dot(attention_rows, out_weight, preferred_element_type=jnp.float32)  15 us
  transfers between devices with their start and end apart: 32, of which 17 were waited for; matrix products, arithmetic and copies ran while one was open for 0% of the time, Pallas kernels for 0%

commit v1 on v0

v1 whole, which is shorter than its diff:
```python
import functools
import math

import jax
import jax.numpy as jnp
from jax import lax
from jax.experimental import pallas as pl
from jax.experimental.pallas import tpu as pltpu
from jax.sharding import PartitionSpec as P

HD = 128
BLOCK = 64
QUANT_STEP = 1.0 / 2048.0
MASKED = -1e30
LANES = 128


def hadamard_signs(size_value):
    indices = jnp.arange(size_value, dtype=jnp.int32)
    common = jnp.bitwise_and(indices[:, None], indices[None, :])
    parity = jnp.zeros((size_value, size_value), jnp.int32)
    for shift_bit in range(max(int(size_value).bit_length(), 1)):
        parity = jnp.bitwise_xor(parity, jnp.bitwise_and(jnp.right_shift(common, shift_bit), 1))
    return 1.0 - 2.0 * parity.astype(jnp.float32)


def attend_kernel(heads, group, q_ref, kk_ref, vv_ref, scale_ref, pos_ref, o_ref, top_ref, total_ref, s_a, s_b):
    rows, ctx = s_a.shape
    lane = lax.broadcasted_iota(jnp.int32, (rows, LANES), 1)

    def scores(h, s_ref):
        g = h // group
        col = pl.multiple_of(h * HD, HD)
        q = q_ref[:, pl.ds(col, HD)]
        s = jnp.dot(jnp.concatenate([q, q], axis=1), kk_ref[g], preferred_element_type=jnp.float32)
        where = lax.broadcasted_iota(jnp.int32, (rows, ctx), 1)
        s = jnp.where(where <= pos_ref[...], s * scale_ref[g], MASKED)
        s_ref[...] = s
        return jnp.max(s, axis=1, keepdims=True)

    def values(h, s_ref, top):
        g = h // group
        col = pl.multiple_of(h * HD, HD)
        p = jnp.exp2(s_ref[...] - top).astype(jnp.bfloat16)
        both = jnp.dot(p, vv_ref[g], preferred_element_type=jnp.float32)
        total = both[:, HD:]
        o_ref[:, pl.ds(col, HD)] = (both[:, :HD] / total).astype(jnp.bfloat16)
        top_ref[...] = jnp.where(lane == h, top, top_ref[...])
        total_ref[...] = jnp.where(lane == h, total, total_ref[...])

    top_ref[...] = jnp.zeros_like(top_ref)
    total_ref[...] = jnp.zeros_like(total_ref)
    first = scores(0, s_a)

    def step(i, top_a):
        h = i * 2
        top_b = scores(h + 1, s_b)
        values(h, s_a, top_a)
        later = scores(jnp.minimum(h + 2, heads - 1), s_a)
        values(h + 1, s_b, top_b)
        return later

    lax.fori_loop(0, heads // 2, step, first)


def attend(queries, kk, vv, scale, limit, heads, group):
    rows, width = queries.shape
    kv, depth, ctx = kk.shape
    block = min(256, rows)
    whole = lambda r: (0, 0, 0)
    stats = jax.ShapeDtypeStruct((rows, LANES), jnp.float32)
    return pl.pallas_call(
        functools.partial(attend_kernel, heads, group),
        grid=(rows // block,),
        in_specs=[
            pl.BlockSpec((block, width), lambda r: (r, 0)),
            pl.BlockSpec((kv, depth, ctx), whole),
            pl.BlockSpec((kv, ctx, 2 * HD), whole),
            pl.BlockSpec((kv, 1, ctx), whole),
            pl.BlockSpec((block, 1), lambda r: (r, 0)),
        ],
        out_specs=[
            pl.BlockSpec((block, width), lambda r: (r, 0)),
            pl.BlockSpec((block, LANES), lambda r: (r, 0)),
            pl.BlockSpec((block, LANES), lambda r: (r, 0)),
        ],
        out_shape=[jax.ShapeDtypeStruct((rows, width), jnp.bfloat16), stats, stats],
        scratch_shapes=[pltpu.VMEM((block, ctx), jnp.float32)] * 2,
        compiler_params=pltpu.CompilerParams(vmem_limit_bytes=48 * 1024 * 1024),
        cost_estimate=pl.CostEstimate(
            flops=6 * rows * width * ctx, bytes_accessed=4 * rows * width, transcendentals=rows * heads * ctx
        ),
    )(queries, kk, vv, scale, limit)


def on_device(queries, key_codes, value_codes, key_scales, value_scales, positions, out_weight):
    q_rows = queries.shape[0]
    kv_local = key_scales.shape[1]
    ctx_local = key_codes.shape[0]
    heads_local = queries.shape[1] // HD
    group_size = heads_local // kv_local
    cycle_index = lax.axis_index("ctx")
    cycle_size = lax.axis_size("ctx")
    signs = hadamard_signs(HD)
    every_query = lax.all_gather(queries, "ctx", axis=0, tiled=True)
    keys = key_codes.reshape(ctx_local, kv_local, HD)
    turned = jnp.einsum(
        "cgd,de->gec", keys, signs.astype(jnp.bfloat16), preferred_element_type=jnp.float32
    )
    coarse = jnp.floor(turned * (1.0 / 128.0)) * 128.0
    kk = jnp.concatenate([coarse, turned - coarse], axis=1).astype(jnp.bfloat16)
    scale = jnp.repeat(key_scales.astype(jnp.float32), BLOCK, axis=0).T[:, None, :]
    scale = scale * (QUANT_STEP / HD * math.log2(math.e))
    value_factor = jnp.repeat(value_scales.astype(jnp.float32), BLOCK, axis=0) * QUANT_STEP
    scaled = value_codes.reshape(ctx_local, kv_local, HD).astype(jnp.float32) * value_factor[..., None]
    vv = jnp.concatenate([scaled, jnp.ones_like(scaled)], axis=2).astype(jnp.bfloat16)
    vv = vv.transpose(1, 0, 2)
    limit = (positions - cycle_index * ctx_local)[:, None]
    part, top, total = attend(every_query, kk, vv, scale, limit, heads_local, group_size)

    part = lax.all_to_all(part, "ctx", 0, 0, tiled=True).reshape(cycle_size, q_rows, heads_local, HD)
    stats = jnp.concatenate([top[:, :heads_local], total[:, :heads_local]], axis=1)
    stats = lax.all_to_all(stats, "ctx", 0, 0, tiled=True).reshape(cycle_size, q_rows, 2, heads_local)
    top, total = stats[:, :, 0], stats[:, :, 1]
    share = total * jnp.exp2(top - jnp.max(top, axis=0, keepdims=True))
    share = share / jnp.sum(share, axis=0, keepdims=True)
    normalized = jnp.sum(part.astype(jnp.float32) * share[..., None], axis=0).astype(jnp.bfloat16)
    restored = jnp.einsum(
        "rhd,de->rhe", normalized, signs.astype(jnp.bfloat16), preferred_element_type=jnp.float32
    )
    attention = (restored / math.sqrt(HD)).astype(jnp.bfloat16).reshape(q_rows, heads_local * HD)
    attention_rows = lax.all_gather(attention, "ctx", axis=0, tiled=True)
    projected = lax.psum_scatter(
        jnp.dot(attention_rows, out_weight, preferred_element_type=jnp.float32),
        "head",
        scatter_dimension=0,
        tiled=True,
    )
    return projected.astype(jnp.bfloat16)


def solution(mesh):
    in_specs = (
        P("ctx", "head"),
        P("ctx", "head"),
        P("ctx", "head"),
        P("ctx", "head"),
        P("ctx", "head"),
        P(),
        P("head", "ctx"),
    )
    out_specs = P("head", "ctx")
    return jax.shard_map(
        on_device, mesh=mesh, in_specs=in_specs, out_specs=out_specs, check_vma=False
    )
```

time: 595 us -> 357 us (0.60)
  matrix products: 192 us -> 15.9 us
  Pallas kernels: 0 us -> 59 us
  waiting for transfers between devices: 262 us -> 215 us
  starting transfers between devices: 45.9 us -> 6.08 us
  other arithmetic: 50.5 us -> 13.3 us
  blocking collectives: 0 us -> 9.53 us
    dot_general x18 -> x2, matrix products: 177 us -> 0.92 us  [the longest x1 0.58 us: on_device(): jnp.einsum('cgd,de->gec', keys, signs.astype(jnp.bfloat16), preferred_ele...]
    ppermute x30 -> x0, waiting for transfers between devices: 150 us -> none  [shifted(): return lax.ppermute(value, axis, pairs)]
    all_to_all x0 -> x1, waiting for transfers between devices: none -> 74.7 us  [on_device(): lax.all_to_all(part, 'ctx', 0, 0, tiled=True)]
    pallas_call x0 -> x1, Pallas kernels: none -> 59 us  [attend(): pl.pallas_call(functools.partial(attend_kernel, heads, group), grid=(rows...]
    ppermute x30 -> x0, starting transfers between devices: 45.9 us -> none  [shifted(): return lax.ppermute(value, axis, pairs)]
    reduce_sum x8 -> x2, other arithmetic: 46.4 us -> 5.75 us  [the longest x1 5.71 us: on_device(): jnp.sum(part.astype(jnp.float32) * share[..., None], axis=0)]
    all_gather x0 -> x1, waiting for transfers between devices: none -> 39.5 us  [on_device(): every_query = lax.all_gather(queries, 'ctx', axis=0, tiled=True)]
    mul x8 -> x4, local copies, waits for them, and re-layouts: 0.69 us -> 14 us  [the longest x2 13.9 us: on_device(): part.astype(jnp.float32) * share[..., None]]
  transfers between devices with their start and end apart: 32 -> 4, of which waited for: 17 -> 4; matrix products, arithmetic and copies ran while one was open for 0% -> 7% of each run, Pallas kernels for 0% -> 0%
where the time goes in v1:
time: 357 us; the launch traced here: 355 us
  waiting for transfers between devices  215 us (60%)
  Pallas kernels  59 us (17%)
  local copies, waits for them, and re-layouts  22.1 us (6%)
  matrix products  15.9 us (4%)
  other arithmetic  13.3 us (4%)
  between operations  13.3 us (4%)
  blocking collectives  9.53 us (3%)
  starting transfers between devices  6.08 us (2%)
    all_to_all x1, waiting for transfers between devices, on_device(): lax.all_to_all(part, 'ctx', 0, 0, tiled=True)  74.7 us
    pallas_call x1, Pallas kernels, attend(): pl.pallas_call(functools.partial(attend_kernel, heads, group), grid=(rows...  59 us
    reduce_scatter x1, waiting for transfers between devices, on_device(): lax.psum_scatter(jnp.dot(attention_rows, out_weight, preferred_element_ty...  52.7 us
    all_gather x1, waiting for transfers between devices, on_device(): attention_rows = lax.all_gather(attention, 'ctx', axis=0, tiled=True)  47.8 us
    all_gather x1, waiting for transfers between devices, on_device(): every_query = lax.all_gather(queries, 'ctx', axis=0, tiled=True)  39.5 us
    dot_general x1, matrix products, on_device(): jnp.dot(attention_rows, out_weight, preferred_element_type=jnp.float32)  15 us
    mul x2, local copies, waits for them, and re-layouts, on_device(): part.astype(jnp.float32) * share[..., None]  13.9 us
    all_to_all x1, blocking collectives, on_device(): lax.all_to_all(stats, 'ctx', 0, 0, tiled=True)  9.53 us
  transfers between devices with their start and end apart: 4, of which 4 were waited for; matrix products, arithmetic and copies ran while one was open for 7% of the time, Pallas kernels for 0%

profile of v1, /device:TPU:9, one launch (start us, length us, event | category | flops | bytes accessed | tf_op | source)
XLA Modules:
  0.0 354.6 jit_solution(5093888403180372904)
XLA Ops:
  6.5 0.0 copy-start
  6.5 0.0 all-gather.3.cloned.1.call-start
  6.5 0.7 all-gather.3.cloned.1.call-update
  7.3 0.7 convert_multiply_fusion.1
  7.9 0.1 broadcast_in_dim.6
  8.0 0.1 mul.83
  8.1 0.7 convert_multiply_fusion
  8.8 0.1 broadcast_in_dim.7
  8.9 0.1 mul.88
  9.0 0.7 broadcast_subtract_fusion
  9.7 0.1 copy.15.pos_ref
  9.8 2.3 copy.13
  12.1 1.5 copy.14
  13.6 0.7 multiply_convert_fusion
  14.3 0.2 pad_bitcast_fusion.vv_ref
  14.5 0.0 copy-done
  14.5 0.6 fusion
  15.1 1.6 pad_maximum_fusion.kk_ref
  16.7 39.5 %all-gather.3.cloned.1.call-done.q_ref = bf16[512,4096]{1,0:T(8,128)(2,1)} async-done(((bf16[64,4096]{1,0:T(8,128)(2,1)}), bf16[512,4096]{1,0:T(8,128)(2,1)}) %all-gather.3.cloned.1.call-update) | async-done | bytes 4194320 | tf_op jit(solution)/shard_map/all_gather | solution.py:105
  56.2 0.0 copy-start.2
  56.2 1.6 copy-done.2
  57.8 59.0 %shard_map.73 = (bf16[512,4096]{1,0:T(8,128)(2,1)}, f32[512,128]{1,0:T(8,128)S(1)}, f32[512,128]{1,0:T(8,128)S(1)}) custom-call(bf16[512,4096]{1,0:T(8,128)(2,1)} %all-gather.3.cloned.1.call-done.q_ref, bf16[2,256,2048]{2,1,0:T(8,128)(2,1)S(1)} %copy-done.2, bf16[2,2048,256]{2,1,0:T(8,128)(2,1)S(1)} %pad_bitcast_fusion.vv_ref, ...), custom_call_target="tpu_custom_call" | custom-call | flops 25769803776 | bytes 8388608 | tf_op jit(solution)/shard_map/pallas_call | solution.py:72
  116.7 0.1 pad_maximum_fusion.1
  116.9 0.1 copy.16
  117.0 0.2 reshape.55
  117.2 9.5 %all_to_all.18 = f32[8,1,4096]{2,1,0:T(1,128)S(1)} all-to-all(f32[8,1,4096]{2,1,0:T(1,128)S(1)} %reshape.55), channel_id=1, replica_groups=mesh['ctx'=8,'head'=4] {'ctx'}, dimensions={0} | all-to-all | bytes 262144 | tf_op jit(solution)/shard_map/all_to_all | solution.py:123
  126.7 6.0 %all-to-all-start = ((bf16[8,64,4096]{2,1,0:T(8,128)(2,1)}), bf16[8,64,4096]{2,1,0:T(8,128)(2,1)}, u32[]{:S(2)}, u32[]{:S(2)}) async-start(bf16[8,64,4096]{2,1,0:T(8,128)(2,1)} %bitcast.73), calls=%async_computation | async-start | bytes 8388608 | tf_op jit(solution)/shard_map/all_to_all | solution.py:121
  132.8 0.0 all-gather.5.cloned.1.call-start
  132.8 0.5 broadcast.47
  133.3 1.0 reduce.2
  134.2 0.1 reshape.56
  134.5 0.1 copy.18
  134.6 4.6 %mul.93 = f32[8,64,32,128]{3,2,1,0:T(8,128)} broadcast(f32[8,64,32]{2,1,0:T(8,128)S(1)} %copy.18), dimensions={0,1,2} | broadcast | bytes 8454144 | tf_op jit(solution)/shard_map/mul | solution.py:127
  139.2 9.4 %mul.94 = f32[8,64,4096]{2,1,0:T(8,128)} reshape(f32[8,64,32,128]{3,2,1,0:T(8,128)} %mul.93) | data formatting | bytes 16777216 | tf_op jit(solution)/shard_map/mul | solution.py:127
  148.5 74.7 %all-to-all-done = bf16[8,64,4096]{2,1,0:T(8,128)(2,1)} async-done(((bf16[8,64,4096]{2,1,0:T(8,128)(2,1)}), bf16[8,64,4096]{2,1,0:T(8,128)(2,1)}, u32[]{:S(2)}, u32[]{:S(2)}) %all-to-all-start) | async-done | bytes 4194336 | tf_op jit(solution)/shard_map/all_to_all | solution.py:121
  223.2 5.7 %multiply_reduce_fusion = bf16[64,4096]{1,0:T(8,128)(2,1)S(1)} fusion(f32[8,64,4096]{2,1,0:T(8,128)} %mul.94, bf16[8,64,4096]{2,1,0:T(8,128)(2,1)} %all-to-all-done), kind=kLoop, calls=%fused_computation | loop fusion | flops 6029312 | bytes 13107200 | tf_op jit(solution)/shard_map/reduce_sum | solution.py:127
  228.9 0.1 copy.23
  229.0 0.3 fusion.1
  229.4 1.0 copy.32
  230.4 0.0 all-gather.5.cloned.1.call-update
  230.4 0.0 reduce-scatter.2.cloned.1.call-start
  230.5 47.8 %all-gather.5.cloned.1.call-done = bf16[512,4096]{1,0:T(8,128)(2,1)} async-done(((bf16[64,4096]{1,0:T(8,128)(2,1)}), bf16[512,4096]{1,0:T(8,128)(2,1)}) %all-gather.5.cloned.1.call-update) | async-done | bytes 4194320 | tf_op jit(solution)/shard_map/all_gather | solution.py:132
  278.2 0.0 copy-start.1
  278.2 15.0 %fusion.37 = f32[512,2048]{1,0:T(8,128)} fusion(bf16[512,4096]{1,0:T(8,128)(2,1)} %all-gather.5.cloned.1.call-done, bf16[4096,2048]{1,0:T(8,128)(2,1)} %param.13), kind=kOutput, calls=%fused_computation.54 | convolution fusion | flops 8589934592 | bytes 25165824 | tf_op jit(solution)/shard_map/dot_general | solution.py:134
  293.2 0.0 reduce-scatter.2.cloned.1.call-update
  293.3 52.7 %reduce-scatter.2.cloned.1.call-done = f32[128,2048]{1,0:T(8,128)} async-done(((f32[512,2048]{1,0:T(8,128)}), f32[128,2048]{1,0:T(8,128)}) %reduce-scatter.2.cloned.1.call-update) | async-done | bytes 1048592 | tf_op jit(solution)/shard_map/reduce_scatter | solution.py:133
  346.0 2.1 convert_element_type.51
  348.0 0.0 copy-done.1
  (4 shorter events, 0.1 us)
Async XLA Ops:
  6.5 8.0 %copy-start = (bf16[2048,256]{1,0:T(8,128)(2,1)S(1)}, bf16[2048,256]{1,0:T(8,128)(2,1)}, u32[]{:S(2)}) copy-start(bf16[2048,256]{1,0:T(8,128)(2,1)} %param.8) | copy-start | bytes 3145732
  6.5 49.6 %all-gather.3.cloned.1.call-start = ((), (), s32[]{:S(2)}) async-start(), calls=%async_computation.3 | async-start | bytes 4718592 | tf_op jit(solution)/shard_map/all_gather | solution.py:105
  56.2 1.6 copy-start.2
  126.7 96.5 %all-to-all-start = ((bf16[8,64,4096]{2,1,0:T(8,128)(2,1)}), bf16[8,64,4096]{2,1,0:T(8,128)(2,1)}, u32[]{:S(2)}, u32[]{:S(2)}) async-start(bf16[8,64,4096]{2,1,0:T(8,128)(2,1)} %bitcast.73), calls=%async_computation | async-start | bytes 8388608 | tf_op jit(solution)/shard_map/all_to_all | solution.py:121
  132.8 145.5 %all-gather.5.cloned.1.call-start = ((), (), s32[]{:S(2)}) async-start(), calls=%async_computation.4 | async-start | bytes 4718592 | tf_op jit(solution)/shard_map/all_gather | solution.py:132
  230.4 115.5 %reduce-scatter.2.cloned.1.call-start = ((), (), s32[]{:S(2)}) async-start(), calls=%async_computation.5 | async-start | bytes 5242880 | tf_op jit(solution)/shard_map/reduce_scatter | solution.py:133
  278.2 69.8 %copy-start.1 = (bf16[2048,256]{1,0:T(8,128)(2,1)S(1)}, bf16[2048,256]{1,0:T(8,128)(2,1)}, u32[]{:S(2)}) copy-start(bf16[2048,256]{1,0:T(8,128)(2,1)} %param.8) | copy-start | bytes 3145732
Sparse Core Ops, SparseCore 0:
  9.0 47.1 all-gather.2
  230.5 47.6 all-gather.4
  293.4 52.5 reduce-scatter.1

commit v2 on v1

--- a/solution.py
+++ b/solution.py
@@ -13,6 +13,7 @@
 QUANT_STEP = 1.0 / 2048.0
 MASKED = -1e30
 LANES = 128
+MESH = pl.DeviceIdType.MESH
 
 
 def hadamard_signs(size_value):
@@ -93,6 +94,136 @@
     )(queries, kk, vv, scale, limit)
 
 
+def project_kernel(chips, parts, a_ref, w_hbm, o_ref, w_ref, att, own, out_part, in_part,
+                   w_sem, send_z, recv_z, send_core, recv_core, send_head, recv_head):
+    me = lax.axis_index("ctx")
+    mine = lax.axis_index("head")
+    chip, core = me // 2, lax.rem(me, 2)
+    sibling = chip * 2 + 1 - core
+    half = a_ref.shape[1]
+    columns = w_ref.shape[1]
+    tile = min(512, columns)
+    load = pltpu.make_async_copy(w_hbm, w_ref, w_sem)
+    load.start()
+
+    barrier = pltpu.get_barrier_semaphore()
+    pl.semaphore_signal(barrier, inc=1, device_id={"ctx": sibling}, device_id_type=MESH)
+    for k in range(1, chips):
+        other = lax.rem(chip + k, chips) * 2 + core
+        pl.semaphore_signal(barrier, inc=1, device_id={"ctx": other}, device_id_type=MESH)
+    for k in range(1, parts):
+        other = lax.rem(mine + k, parts)
+        pl.semaphore_signal(barrier, inc=1, device_id={"head": other}, device_id_type=MESH)
+    pl.semaphore_wait(barrier, chips + parts - 1)
+
+    def to_chip(k):
+        return pltpu.make_async_remote_copy(
+            src_ref=a_ref, dst_ref=att.at[chip, core],
+            send_sem=send_z.at[k], recv_sem=recv_z.at[chips - k],
+            device_id={"ctx": lax.rem(chip + k, chips) * 2 + core}, device_id_type=MESH)
+
+    def from_chip(k):
+        source = lax.rem(chip + k, chips)
+        return pltpu.make_async_remote_copy(
+            src_ref=a_ref, dst_ref=att.at[source, core],
+            send_sem=send_z.at[k], recv_sem=recv_z.at[k],
+            device_id={"ctx": source * 2 + core}, device_id_type=MESH)
+
+    def to_core(k):
+        source = lax.rem(chip + k, chips)
+        return pltpu.make_async_remote_copy(
+            src_ref=a_ref if k == 0 else att.at[source, core], dst_ref=att.at[source, core],
+            send_sem=send_core.at[k], recv_sem=recv_core.at[k],
+            device_id={"ctx": sibling}, device_id_type=MESH)
+
+    def from_core(k):
+        source = lax.rem(chip + k, chips)
+        return pltpu.make_async_remote_copy(
+            src_ref=a_ref, dst_ref=att.at[source, 1 - core],
+            send_sem=send_core.at[k], recv_sem=recv_core.at[k],
+            device_id={"ctx": sibling}, device_id_type=MESH)
+
+    def to_part(k):
+        block = lax.rem(chip + k, chips)
+        return pltpu.make_async_remote_copy(
+            src_ref=out_part.at[k], dst_ref=in_part.at[mine],
+            send_sem=send_head.at[k], recv_sem=recv_head.at[mine],
+            device_id={"head": block}, device_id_type=MESH)
+
+    for k in range(1, chips):
+        to_chip(k).start()
+    to_core(0).start()
+    att[chip, core] = a_ref[...]
+    load.wait()
+    for k in range(chips):
+        if k > 0:
+            from_chip(k).wait_recv()
+            to_core(k).start()
+        from_core(k).wait_recv()
+        block = lax.rem(chip + k, chips)
+
+        @pl.loop(0, columns // tile)
+        def _(t):
+            cols = pl.ds(pl.multiple_of(t * tile, tile), tile)
+            product = jnp.dot(att[block, 0], w_ref[:half, cols], preferred_element_type=jnp.float32)
+            product += jnp.dot(att[block, 1], w_ref[half:, cols], preferred_element_type=jnp.float32)
+            out_part[k, :, cols] = product.astype(jnp.bfloat16)
+
+            @pl.when(block == mine)
+            def _():
+                own[:, cols] = product
+
+        @pl.when(block != mine)
+        def _():
+            to_part(k).start()
+
+    total = own[...]
+    for k in range(1, parts):
+        source = lax.rem(mine + k, parts)
+        pltpu.make_async_remote_copy(
+            src_ref=out_part.at[0], dst_ref=in_part.at[source],
+            send_sem=send_head.at[0], recv_sem=recv_head.at[source],
+            device_id={"head": source}, device_id_type=MESH).wait_recv()
+        total = total + in_part[source].astype(jnp.float32)
+    o_ref[...] = total.astype(o_ref.dtype)
+    for k in range(1, chips):
+        to_chip(k).wait_send()
+    for k in range(chips):
+        to_core(k).wait_send()
+
+        @pl.when(lax.rem(chip + k, chips) != mine)
+        def _():
+            to_part(k).wait_send()
+
+
+def project(piece, out_weight, chips, parts):
+    rows, half = piece.shape
+    depth, columns = out_weight.shape
+    dma = pltpu.SemaphoreType.DMA
+    return pl.pallas_call(
+        functools.partial(project_kernel, chips, parts),
+        out_shape=jax.ShapeDtypeStruct((rows, columns), jnp.bfloat16),
+        in_specs=[pl.BlockSpec(memory_space=pltpu.VMEM), pl.BlockSpec(memory_space=pl.ANY)],
+        out_specs=pl.BlockSpec(memory_space=pltpu.VMEM),
+        scratch_shapes=[
+            pltpu.VMEM((depth, columns), jnp.bfloat16),
+            pltpu.VMEM((chips, 2, rows, half), jnp.bfloat16),
+            pltpu.VMEM((rows, columns), jnp.float32),
+            pltpu.VMEM((chips, rows, columns), jnp.bfloat16),
+            pltpu.VMEM((parts, rows, columns), jnp.bfloat16),
+            dma,
+            dma((chips,)), dma((chips,)), dma((chips,)), dma((chips,)),
+            dma((chips,)), dma((parts,)),
+        ],
+        compiler_params=pltpu.CompilerParams(
+            collective_id=1, has_side_effects=True, vmem_limit_bytes=50 * 1024 * 1024
+        ),
+        cost_estimate=pl.CostEstimate(
+            flops=2 * chips * rows * depth * columns, bytes_accessed=2 * depth * columns, transcendentals=0
+        ),
+    )(piece, out_weight)
+
+
 def on_device(queries, key_codes, value_codes, key_scales, value_scales, positions, out_weight):
     q_rows = queries.shape[0]
     kv_local = key_scales.shape[1]
@@ -129,14 +260,14 @@
         "rhd,de->rhe", normalized, signs.astype(jnp.bfloat16), preferred_element_type=jnp.float32
     )
     attention = (restored / math.sqrt(HD)).astype(jnp.bfloat16).reshape(q_rows, heads_local * HD)
-    attention_rows = lax.all_gather(attention, "ctx", axis=0, tiled=True)
-    projected = lax.psum_scatter(
-        jnp.dot(attention_rows, out_weight, preferred_element_type=jnp.float32),
-        "head",
-        scatter_dimension=0,
-        tiled=True,
-    )
-    return projected.astype(jnp.bfloat16)
+    half = attention.shape[1] // 2
+    core = cycle_index % 2
+    kept = lax.dynamic_slice_in_dim(attention, core * half, half, 1)
+    given = lax.dynamic_slice_in_dim(attention, (1 - core) * half, half, 1)
+    taken = lax.ppermute(given, "ctx", [(i, i ^ 1) for i in range(cycle_size)])
+    pair = jnp.stack([kept, taken])
+    piece = jnp.where(core == 0, pair, pair[::-1]).reshape(2 * q_rows, half)
+    return project(piece, out_weight, cycle_size // 2, lax.axis_size("head"))
 
 
 def solution(mesh):

time: 357 us -> 329 us (0.922)
  waiting for transfers between devices: 215 us -> 118 us
  Pallas kernels: 59 us -> 148 us
  matrix products: 15.9 us -> 0.91 us
  other arithmetic: 13.3 us -> 9.32 us
    pallas_call x0 -> x1, Pallas kernels: none -> 89.3 us  [project(): pl.pallas_call(functools.partial(project_kernel, chips, parts), out_shape...]
    reduce_scatter x1 -> x0, waiting for transfers between devices: 52.7 us -> none  [on_device(): lax.psum_scatter(jnp.dot(attention_rows, out_weight, preferred_element_ty...]
    all_gather x1 -> x0, waiting for transfers between devices: 47.8 us -> none  [on_device(): attention_rows = lax.all_gather(attention, 'ctx', axis=0, tiled=True)]
    dot_general x1 -> x0, matrix products: 15 us -> none  [on_device(): jnp.dot(attention_rows, out_weight, preferred_element_type=jnp.float32)]
  transfers between devices with their start and end apart: 4 -> 3, of which waited for: 4 -> 3; matrix products, arithmetic and copies ran while one was open for 7% -> 7% of each run, Pallas kernels for 0% -> 0%
where the time goes in v2:
time: 329 us; the launch traced here: 328 us
  Pallas kernels  148 us (45%)
  waiting for transfers between devices  118 us (36%)
  local copies, waits for them, and re-layouts  22.2 us (7%)
  between operations  13.6 us (4%)
  blocking collectives  9.54 us (3%)
  other arithmetic  9.32 us (3%)
  starting transfers between devices  6.56 us (2%)
    pallas_call x1, Pallas kernels, project(): pl.pallas_call(functools.partial(project_kernel, chips, parts), out_shape...  89.3 us
    all_to_all x1, waiting for transfers between devices, on_device(): lax.all_to_all(part, 'ctx', 0, 0, tiled=True)  74.7 us
    pallas_call x1, Pallas kernels, attend(): pl.pallas_call(functools.partial(attend_kernel, heads, group), grid=(rows...  59 us
    all_gather x1, waiting for transfers between devices, on_device(): every_query = lax.all_gather(queries, 'ctx', axis=0, tiled=True)  41.4 us
    mul x2, local copies, waits for them, and re-layouts, on_device(): part.astype(jnp.float32) * share[..., None]  13.9 us
    all_to_all x1, blocking collectives, on_device(): lax.all_to_all(stats, 'ctx', 0, 0, tiled=True)  9.54 us
  transfers between devices with their start and end apart: 3, of which 3 were waited for; matrix products, arithmetic and copies ran while one was open for 7% of the time, Pallas kernels for 0%

profile of v2, /device:TPU:9, one launch (start us, length us, event | category | flops | bytes accessed | tf_op | source)
XLA Modules:
  0.0 328.5 jit_solution(11688226857219401536)
XLA Ops:
  6.5 0.0 copy-start
  6.5 0.0 all-gather.2.cloned.1.call-start
  6.5 0.7 all-gather.2.cloned.1.call-update
  7.3 2.3 copy.13
  9.6 0.0 copy-start.3
  9.6 0.0 copy-start.4
  9.6 0.0 copy-start.2
  9.6 1.5 copy.14
  11.1 0.0 copy-done.3
  11.1 0.1 broadcast_in_dim.6
  11.2 0.1 mul.89
  11.3 0.0 copy-done.4
  11.3 0.1 broadcast_in_dim.7
  11.4 0.1 mul.94
  11.5 0.0 copy-done.2
  11.5 0.1 copy.15.pos_ref
  11.7 0.7 multiply_convert_fusion
  12.4 0.2 pad_bitcast_fusion.vv_ref
  12.6 0.0 copy-done
  12.6 0.6 fusion
  13.2 1.6 pad_maximum_fusion.kk_ref
  14.7 41.4 %all-gather.2.cloned.1.call-done.q_ref = bf16[512,4096]{1,0:T(8,128)(2,1)} async-done(((bf16[64,4096]{1,0:T(8,128)(2,1)}), bf16[512,4096]{1,0:T(8,128)(2,1)}) %all-gather.2.cloned.1.call-update) | async-done | bytes 4194320 | tf_op jit(solution)/shard_map/all_gather | solution.py:236
  56.2 0.0 copy-start.1
  56.2 1.6 copy-done.1
  57.8 59.0 %shard_map.73 = (bf16[512,4096]{1,0:T(8,128)(2,1)}, f32[512,128]{1,0:T(8,128)S(1)}, f32[512,128]{1,0:T(8,128)S(1)}) custom-call(bf16[512,4096]{1,0:T(8,128)(2,1)} %all-gather.2.cloned.1.call-done.q_ref, bf16[2,256,2048]{2,1,0:T(8,128)(2,1)S(1)} %copy-done.1, bf16[2,2048,256]{2,1,0:T(8,128)(2,1)S(1)} %pad_bitcast_fusion.vv_ref, ...), custom_call_target="tpu_custom_call" | custom-call | flops 25769803776 | bytes 8388608 | tf_op jit(solution)/shard_map/pallas_call | solution.py:73
  116.8 0.1 pad_maximum_fusion.2
  116.9 0.1 copy.16
  117.0 0.2 reshape.59
  117.2 9.5 %all_to_all.18 = f32[8,1,4096]{2,1,0:T(1,128)S(1)} all-to-all(f32[8,1,4096]{2,1,0:T(1,128)S(1)} %reshape.59), channel_id=1, replica_groups=mesh['ctx'=8,'head'=4] {'ctx'}, dimensions={0} | all-to-all | bytes 262144 | tf_op jit(solution)/shard_map/all_to_all | solution.py:254
  126.8 6.0 %all-to-all-start = ((bf16[8,64,4096]{2,1,0:T(8,128)(2,1)}), bf16[8,64,4096]{2,1,0:T(8,128)(2,1)}, u32[]{:S(2)}, u32[]{:S(2)}) async-start(bf16[8,64,4096]{2,1,0:T(8,128)(2,1)} %bitcast.76), calls=%async_computation | async-start | bytes 8388608 | tf_op jit(solution)/shard_map/all_to_all | solution.py:252
  132.8 0.5 broadcast.48
  133.3 1.0 reduce.2
  134.3 0.1 reshape.60
  134.5 0.1 copy.18
  134.6 4.5 %mul.99 = f32[8,64,32,128]{3,2,1,0:T(8,128)} broadcast(f32[8,64,32]{2,1,0:T(8,128)S(1)} %copy.18), dimensions={0,1,2} | broadcast | bytes 8454144 | tf_op jit(solution)/shard_map/mul | solution.py:258
  139.2 9.4 %mul.100 = f32[8,64,4096]{2,1,0:T(8,128)} reshape(f32[8,64,32,128]{3,2,1,0:T(8,128)} %mul.99) | data formatting | bytes 16777216 | tf_op jit(solution)/shard_map/mul | solution.py:258
  148.6 74.7 %all-to-all-done = bf16[8,64,4096]{2,1,0:T(8,128)(2,1)} async-done(((bf16[8,64,4096]{2,1,0:T(8,128)(2,1)}), bf16[8,64,4096]{2,1,0:T(8,128)(2,1)}, u32[]{:S(2)}, u32[]{:S(2)}) %all-to-all-start) | async-done | bytes 4194336 | tf_op jit(solution)/shard_map/all_to_all | solution.py:252
  223.2 5.7 %multiply_reduce_fusion = bf16[64,4096]{1,0:T(8,128)(2,1)S(1)} fusion(f32[8,64,4096]{2,1,0:T(8,128)} %mul.100, bf16[8,64,4096]{2,1,0:T(8,128)(2,1)} %all-to-all-done), kind=kLoop, calls=%fused_computation | loop fusion | flops 6029312 | bytes 13107200 | tf_op jit(solution)/shard_map/reduce_sum | solution.py:258
  229.0 0.1 copy.23
  229.1 0.3 fusion.1
  229.4 0.2 copy.32
  229.7 0.5 collective-permute-start
  230.2 1.2 collective-permute-done
  231.3 0.1 pad_maximum_fusion.1
  231.4 0.1 reverse_select_fusion
  231.5 89.3 %shard_map.74 = bf16[128,2048]{1,0:T(8,128)(2,1)S(1)} custom-call(bf16[128,2048]{1,0:T(8,128)(2,1)S(1)} %bitcast.72, bf16[4096,2048]{1,0:T(8,128)(2,1)} %w_hbm.1), custom_call_target="tpu_custom_call" | custom-call | flops 8589934592 | bytes 16777216 | tf_op jit(solution)/shard_map/pallas_call | solution.py:203
  320.8 0.8 copy.34
  (8 shorter events, 0.2 us)
Async XLA Ops:
  6.5 6.0 %copy-start = (bf16[2048,256]{1,0:T(8,128)(2,1)S(1)}, bf16[2048,256]{1,0:T(8,128)(2,1)}, u32[]{:S(2)}) copy-start(bf16[2048,256]{1,0:T(8,128)(2,1)} %param.8) | copy-start | bytes 3145732
  6.5 49.6 %all-gather.2.cloned.1.call-start = ((), (), s32[]{:S(2)}) async-start(), calls=%async_computation.2 | async-start | bytes 4718592 | tf_op jit(solution)/shard_map/all_gather | solution.py:236
  9.6 1.5 copy-start.3
  9.6 1.7 copy-start.4
  9.6 1.9 copy-start.2
  56.2 1.6 copy-start.1
  126.8 96.5 %all-to-all-start = ((bf16[8,64,4096]{2,1,0:T(8,128)(2,1)}), bf16[8,64,4096]{2,1,0:T(8,128)(2,1)}, u32[]{:S(2)}, u32[]{:S(2)}) async-start(bf16[8,64,4096]{2,1,0:T(8,128)(2,1)} %bitcast.76), calls=%async_computation | async-start | bytes 8388608 | tf_op jit(solution)/shard_map/all_to_all | solution.py:252
  229.7 1.7 collective-permute-start
Sparse Core Ops, SparseCore 0:
  9.0 47.1 all-gather.1

commit v3 on v2

--- a/solution.py
+++ b/solution.py
@@ -25,73 +25,176 @@
     return 1.0 - 2.0 * parity.astype(jnp.float32)
 
 
-def attend_kernel(heads, group, q_ref, kk_ref, vv_ref, scale_ref, pos_ref, o_ref, top_ref, total_ref, s_a, s_b):
-    rows, ctx = s_a.shape
+def attend_kernel(chips, heads, group, q_ref, kk_ref, vv_ref, scale_ref, pos_ref, signs_ref, a_ref,
+                  q_in, s_a, s_b, out_part, in_part, out_stat, in_stat,
+                  send_q, recv_q, send_part, recv_part, send_stat, recv_stat):
+    me = lax.axis_index("ctx")
+    chip, core = me // 2, lax.rem(me, 2)
+    sibling = chip * 2 + 1 - core
+    q_rows = q_ref.shape[0]
+    rows, half = a_ref.shape
+    ctx = s_a.shape[1]
     lane = lax.broadcasted_iota(jnp.int32, (rows, LANES), 1)
 
-    def scores(h, s_ref):
-        g = h // group
-        col = pl.multiple_of(h * HD, HD)
-        q = q_ref[:, pl.ds(col, HD)]
-        s = jnp.dot(jnp.concatenate([q, q], axis=1), kk_ref[g], preferred_element_type=jnp.float32)
-        where = lax.broadcasted_iota(jnp.int32, (rows, ctx), 1)
-        s = jnp.where(where <= pos_ref[...], s * scale_ref[g], MASKED)
-        s_ref[...] = s
-        return jnp.max(s, axis=1, keepdims=True)
-
-    def values(h, s_ref, top):
-        g = h // group
-        col = pl.multiple_of(h * HD, HD)
-        p = jnp.exp2(s_ref[...] - top).astype(jnp.bfloat16)
-        both = jnp.dot(p, vv_ref[g], preferred_element_type=jnp.float32)
-        total = both[:, HD:]
-        o_ref[:, pl.ds(col, HD)] = (both[:, :HD] / total).astype(jnp.bfloat16)
-        top_ref[...] = jnp.where(lane == h, top, top_ref[...])
-        total_ref[...] = jnp.where(lane == h, total, total_ref[...])
-
-    top_ref[...] = jnp.zeros_like(top_ref)
-    total_ref[...] = jnp.zeros_like(total_ref)
-    first = scores(0, s_a)
-
-    def step(i, top_a):
-        h = i * 2
-        top_b = scores(h + 1, s_b)
-        values(h, s_a, top_a)
-        later = scores(jnp.minimum(h + 2, heads - 1), s_a)
-        values(h + 1, s_b, top_b)
-        return later
-
-    lax.fori_loop(0, heads // 2, step, first)
-
-
-def attend(queries, kk, vv, scale, limit, heads, group):
-    rows, width = queries.shape
+    barrier = pltpu.get_barrier_semaphore()
+    for k in range(1, 2 * chips):
+        other = lax.rem(me + k, 2 * chips)
+        pl.semaphore_signal(barrier, inc=1, device_id={"ctx": other}, device_id_type=MESH)
+    pl.semaphore_wait(barrier, 2 * chips - 1)
+
+    def own_rows(which):
+        return pl.ds(pl.multiple_of(which * q_rows, q_rows), q_rows)
+
+    def columns(which):
+        return pl.ds(pl.multiple_of(which * half, half), half)
+
+    def query_out(k, j):
+        there = core if j == 0 else 1 - core
+        return pltpu.make_async_remote_copy(
+            src_ref=q_ref.at[:, columns(there)], dst_ref=q_in.at[chip, own_rows(core)],
+            send_sem=send_q.at[k, j], recv_sem=recv_q.at[lax.rem(chips - k, chips), j],
+            device_id={"ctx": lax.rem(chip + k, chips) * 2 + there}, device_id_type=MESH)
+
+    def query_in(k, j):
+        there = core if j == 0 else 1 - core
+        source = lax.rem(chip + k, chips)
+        return pltpu.make_async_remote_copy(
+            src_ref=q_ref.at[:, columns(core)], dst_ref=q_in.at[source, own_rows(there)],
+            send_sem=send_q.at[k, j], recv_sem=recv_q.at[k, j],
+            device_id={"ctx": source * 2 + there}, device_id_type=MESH)
+
+    def part_out(k):
+        return pltpu.make_async_remote_copy(
+            src_ref=out_part.at[k], dst_ref=in_part.at[lax.rem(chips - k, chips)],
+            send_sem=send_part.at[k], recv_sem=recv_part.at[lax.rem(chips - k, chips)],
+            device_id={"ctx": lax.rem(chip + k, chips) * 2 + core}, device_id_type=MESH)
+
+    def stat_out(k):
+        return pltpu.make_async_remote_copy(
+            src_ref=out_stat.at[k], dst_ref=in_stat.at[lax.rem(chips - k, chips)],
+            send_sem=send_stat.at[k], recv_sem=recv_stat.at[lax.rem(chips - k, chips)],
+            device_id={"ctx": lax.rem(chip + k, chips) * 2 + core}, device_id_type=MESH)
+
+    query_out(0, 1).start()
+    for k in range(1, chips):
+        query_out(k, 0).start()
+        query_out(k, 1).start()
+    q_in[chip, own_rows(core)] = q_ref[:, columns(core)]
+
+    def block(k, carry):
+        query_in(k, 1).wait_recv()
+
+        @pl.when(k > 0)
+        def _():
+            query_in(k, 0).wait_recv()
+
+        source = lax.rem(chip + k, chips)
+        limit = pos_ref[pl.ds(pl.multiple_of(source * rows, rows), rows), :]
+        limit = jnp.concatenate([limit, limit], axis=0)
+
+        def head_columns(h):
+            return pl.ds(pl.multiple_of(h * HD, HD), HD)
+
+        def scores(pair, s_ref):
+            h = pair * 2
+            q = jnp.concatenate([q_in[source, :, head_columns(h)], q_in[source, :, head_columns(h + 1)]], axis=0)
+            g = h // group
+            s = jnp.dot(jnp.concatenate([q, q], axis=1), kk_ref[g], preferred_element_type=jnp.float32)
+            where = lax.broadcasted_iota(jnp.int32, (2 * rows, ctx), 1)
+            s = jnp.where(where <= limit, s * scale_ref[g], MASKED)
+            s_ref[...] = s
+            return jnp.max(s, axis=1, keepdims=True)
+
+        def values(pair, s_ref, top):
+            h = pair * 2
+            g = h // group
+            p = jnp.exp2(s_ref[...] - top).astype(jnp.bfloat16)
+            both = jnp.dot(p, vv_ref[g], preferred_element_type=jnp.float32)
+            total = both[:, HD:]
+            part = (both[:, :HD] / total).astype(jnp.bfloat16)
+            out_part[k, :, head_columns(h)] = part[:rows]
+            out_part[k, :, head_columns(h + 1)] = part[rows:]
+            kept = jnp.where(lane == h, top[:rows], out_stat[k, 0])
+            out_stat[k, 0] = jnp.where(lane == h + 1, top[rows:], kept)
+            kept = jnp.where(lane == h, total[:rows], out_stat[k, 1])
+            out_stat[k, 1] = jnp.where(lane == h + 1, total[rows:], kept)
+
+        out_stat[k] = jnp.ones((2, rows, LANES), jnp.float32)
+        pairs = heads // 2
+
+        def step(i, top_a):
+            top_b = scores(2 * i + 1, s_b)
+            values(2 * i, s_a, top_a)
+            later = scores(2 * i + 2, s_a)
+            values(2 * i + 1, s_b, top_b)
+            return later
+
+        top_a = lax.fori_loop(0, pairs // 2 - 1, step, scores(0, s_a))
+        top_b = scores(pairs - 1, s_b)
+        values(pairs - 2, s_a, top_a)
+        values(pairs - 1, s_b, top_b)
+
+        @pl.when(k > 0)
+        def _():
+            part_out(k).start()
+            stat_out(k).start()
+
+        return carry
+
+    lax.fori_loop(0, chips, block, 0)
+    in_part[0] = out_part[0]
+    in_stat[0] = out_stat[0]
+    for k in range(1, chips):
+        stat_out(chips - k).wait_recv()
+        part_out(chips - k).wait_recv()
+    highest = in_stat[0, 0]
+    for k in range(1, chips):
+        highest = jnp.maximum(highest, in_stat[k, 0])
+    share = [in_stat[k, 1] * jnp.exp2(in_stat[k, 0] - highest) for k in range(chips)]
+    whole = 1.0 / sum(share)
+    share = [one * whole for one in share]
+    for h in range(heads):
+        cols = slice(h * HD, (h + 1) * HD)
+        mixed = sum(in_part[k, :, cols].astype(jnp.float32) * share[k][:, h : h + 1] for k in range(chips))
+        turned = jnp.dot(mixed.astype(jnp.bfloat16), signs_ref[...], preferred_element_type=jnp.float32)
+        a_ref[:, cols] = (turned * (1.0 / math.sqrt(HD))).astype(jnp.bfloat16)
+    query_out(0, 1).wait_send()
+    for k in range(1, chips):
+        query_out(k, 0).wait_send()
+        query_out(k, 1).wait_send()
+        part_out(k).wait_send()
+        stat_out(k).wait_send()
+
+
+def attend(queries, kk, vv, scale, limit, signs, chips, heads, group):
+    q_rows, width = queries.shape
     kv, depth, ctx = kk.shape
-    block = min(256, rows)
-    whole = lambda r: (0, 0, 0)
-    stats = jax.ShapeDtypeStruct((rows, LANES), jnp.float32)
+    rows, half = 2 * q_rows, heads * HD
+    dma = pltpu.SemaphoreType.DMA
     return pl.pallas_call(
-        functools.partial(attend_kernel, heads, group),
-        grid=(rows // block,),
-        in_specs=[
-            pl.BlockSpec((block, width), lambda r: (r, 0)),
-            pl.BlockSpec((kv, depth, ctx), whole),
-            pl.BlockSpec((kv, ctx, 2 * HD), whole),
-            pl.BlockSpec((kv, 1, ctx), whole),
-            pl.BlockSpec((block, 1), lambda r: (r, 0)),
+        functools.partial(attend_kernel, chips, heads, group),
+        in_specs=[pl.BlockSpec(memory_space=pltpu.VMEM)] * 6,
+        out_specs=pl.BlockSpec(memory_space=pltpu.VMEM),
+        out_shape=jax.ShapeDtypeStruct((rows, half), jnp.bfloat16),
+        scratch_shapes=[
+            pltpu.VMEM((chips, rows, half), jnp.bfloat16),
+            pltpu.VMEM((2 * rows, ctx), jnp.float32),
+            pltpu.VMEM((2 * rows, ctx), jnp.float32),
+            pltpu.VMEM((chips, rows, half), jnp.bfloat16),
+            pltpu.VMEM((chips, rows, half), jnp.bfloat16),
+            pltpu.VMEM((chips, 2, rows, LANES), jnp.float32),
+            pltpu.VMEM((chips, 2, rows, LANES), jnp.float32),
+            dma((chips, 2)), dma((chips, 2)),
+            dma((chips,)), dma((chips,)), dma((chips,)), dma((chips,)),
         ],
-        out_specs=[
-            pl.BlockSpec((block, width), lambda r: (r, 0)),
-            pl.BlockSpec((block, LANES), lambda r: (r, 0)),
-            pl.BlockSpec((block, LANES), lambda r: (r, 0)),
-        ],
-        out_shape=[jax.ShapeDtypeStruct((rows, width), jnp.bfloat16), stats, stats],
-        scratch_shapes=[pltpu.VMEM((block, ctx), jnp.float32)] * 2,
-        compiler_params=pltpu.CompilerParams(vmem_limit_bytes=48 * 1024 * 1024),
+        compiler_params=pltpu.CompilerParams(
+            collective_id=0, has_side_effects=True, vmem_limit_bytes=50 * 1024 * 1024
+        ),
         cost_estimate=pl.CostEstimate(
-            flops=6 * rows * width * ctx, bytes_accessed=4 * rows * width, transcendentals=rows * heads * ctx
+            flops=6 * chips * rows * half * ctx, bytes_accessed=4 * q_rows * width,
+            transcendentals=chips * rows * heads * ctx,
         ),
-    )(queries, kk, vv, scale, limit)
+    )(queries, kk, vv, scale, limit, signs)
 
 
 def project_kernel(chips, parts, a_ref, w_hbm, o_ref, w_ref, att, own, out_part, in_part,
@@ -225,48 +328,46 @@
 
 
 def on_device(queries, key_codes, value_codes, key_scales, value_scales, positions, out_weight):
-    q_rows = queries.shape[0]
     kv_local = key_scales.shape[1]
     ctx_local = key_codes.shape[0]
-    heads_local = queries.shape[1] // HD
-    group_size = heads_local // kv_local
     cycle_index = lax.axis_index("ctx")
     cycle_size = lax.axis_size("ctx")
-    signs = hadamard_signs(HD)
-    every_query = lax.all_gather(queries, "ctx", axis=0, tiled=True)
-    keys = key_codes.reshape(ctx_local, kv_local, HD)
+    chip, core = cycle_index // 2, cycle_index % 2
+    heads = queries.shape[1] // HD // 2
+    kv = max(kv_local // 2, 1)
+    swap = [(i, i ^ 1) for i in range(cycle_size)]
+
+    def both_cores(first, second):
+        width = first.shape[1] // kv_local * kv
+
+        def part(value, which):
+            return lax.dynamic_slice_in_dim(value, which * (width if kv_local > 1 else 0), width, 1)
+
+        kept = jnp.concatenate([part(first, core), part(second, core)], axis=1)
+        given = jnp.concatenate([part(first, 1 - core), part(second, 1 - core)], axis=1)
+        taken = lax.ppermute(given, "ctx", swap)
+        low = jnp.where(core == 0, kept, taken)
+        high = jnp.where(core == 0, taken, kept)
+        together = jnp.concatenate([low, high], axis=0)
+        return together[:, :width], together[:, width:]
+
+    ctx = 2 * ctx_local
+    signs = hadamard_signs(HD).astype(jnp.bfloat16)
+    keys, values = both_cores(key_codes, value_codes)
+    key_scales, value_scales = both_cores(key_scales.astype(jnp.float32), value_scales.astype(jnp.float32))
     turned = jnp.einsum(
-        "cgd,de->gec", keys, signs.astype(jnp.bfloat16), preferred_element_type=jnp.float32
+        "cgd,de->gec", keys.reshape(ctx, kv, HD), signs, preferred_element_type=jnp.float32
     )
     coarse = jnp.floor(turned * (1.0 / 128.0)) * 128.0
     kk = jnp.concatenate([coarse, turned - coarse], axis=1).astype(jnp.bfloat16)
-    scale = jnp.repeat(key_scales.astype(jnp.float32), BLOCK, axis=0).T[:, None, :]
+    scale = jnp.repeat(key_scales, BLOCK, axis=0).T[:, None, :]
     scale = scale * (QUANT_STEP / HD * math.log2(math.e))
-    value_factor = jnp.repeat(value_scales.astype(jnp.float32), BLOCK, axis=0) * QUANT_STEP
-    scaled = value_codes.reshape(ctx_local, kv_local, HD).astype(jnp.float32) * value_factor[..., None]
+    value_factor = jnp.repeat(value_scales, BLOCK, axis=0) * QUANT_STEP
+    scaled = values.reshape(ctx, kv, HD).astype(jnp.float32) * value_factor[..., None]
     vv = jnp.concatenate([scaled, jnp.ones_like(scaled)], axis=2).astype(jnp.bfloat16)
     vv = vv.transpose(1, 0, 2)
-    limit = (positions - cycle_index * ctx_local)[:, None]
-    part, top, total = attend(every_query, kk, vv, scale, limit, heads_local, group_size)
-
-    part = lax.all_to_all(part, "ctx", 0, 0, tiled=True).reshape(cycle_size, q_rows, heads_local, HD)
-    stats = jnp.concatenate([top[:, :heads_local], total[:, :heads_local]], axis=1)
-    stats = lax.all_to_all(stats, "ctx", 0, 0, tiled=True).reshape(cycle_size, q_rows, 2, heads_local)
-    top, total = stats[:, :, 0], stats[:, :, 1]
-    share = total * jnp.exp2(top - jnp.max(top, axis=0, keepdims=True))
-    share = share / jnp.sum(share, axis=0, keepdims=True)
-    normalized = jnp.sum(part.astype(jnp.float32) * share[..., None], axis=0).astype(jnp.bfloat16)
-    restored = jnp.einsum(
-        "rhd,de->rhe", normalized, signs.astype(jnp.bfloat16), preferred_element_type=jnp.float32
-    )
-    attention = (restored / math.sqrt(HD)).astype(jnp.bfloat16).reshape(q_rows, heads_local * HD)
-    half = attention.shape[1] // 2
-    core = cycle_index % 2
-    kept = lax.dynamic_slice_in_dim(attention, core * half, half, 1)
-    given = lax.dynamic_slice_in_dim(attention, (1 - core) * half, half, 1)
-    taken = lax.ppermute(given, "ctx", [(i, i ^ 1) for i in range(cycle_size)])
-    pair = jnp.stack([kept, taken])
-    piece = jnp.where(core == 0, pair, pair[::-1]).reshape(2 * q_rows, half)
+    limit = (positions - chip * ctx)[:, None]
+    piece = attend(queries, kk, vv, scale, limit, signs, cycle_size // 2, heads, heads // kv)
     return project(piece, out_weight, cycle_size // 2, lax.axis_size("head"))
 
 

time: 329 us -> 215 us (0.65)
  waiting for transfers between devices: 118 us -> 1.49 us
  Pallas kernels: 148 us -> 201 us
  local copies, waits for them, and re-layouts: 22.2 us -> 5.28 us
  between operations: 13.6 us -> 0.14 us
  blocking collectives: 9.54 us -> 0 us
  starting transfers between devices: 6.56 us -> 1.25 us
  other arithmetic: 9.32 us -> 4.66 us
    all_to_all x1 -> x0, waiting for transfers between devices: 74.7 us -> none  [on_device(): lax.all_to_all(part, 'ctx', 0, 0, tiled=True)]
    pallas_call x1, Pallas kernels: 59 us -> 112 us  [attend(): pl.pallas_call(functools.partial(attend_kernel, chips, heads, group), in_...]
    all_gather x1 -> x0, waiting for transfers between devices: 41.4 us -> none  [on_device(): every_query = lax.all_gather(queries, 'ctx', axis=0, tiled=True)]
    mul x3 -> x1, local copies, waits for them, and re-layouts: 14 us -> 0.08 us  [on_device(): value_factor = jnp.repeat(value_scales, BLOCK, axis=0) * QUANT_STEP]
    all_to_all x1 -> x0, blocking collectives: 9.54 us -> none  [on_device(): lax.all_to_all(stats, 'ctx', 0, 0, tiled=True)]
    all_to_all x1 -> x0, starting transfers between devices: 6.04 us -> none  [on_device(): lax.all_to_all(part, 'ctx', 0, 0, tiled=True)]
    reduce_sum x2 -> x0, other arithmetic: 5.75 us -> none  [the longest x1 5.71 us: on_device(): jnp.sum(part.astype(jnp.float32) * share[..., None], axis=0)]
    mul x1, other arithmetic: 0.01 us -> 3.74 us  [on_device(): values.reshape(ctx, kv, HD).astype(jnp.float32) * value_factor[..., None]]
  transfers between devices with their start and end apart: 3 -> 2, of which waited for: 3 -> 1; matrix products, arithmetic and copies ran while one was open for 7% -> 0% of each run, Pallas kernels for 0% -> 0%
where the time goes in v3:
time: 215 us; the launch traced here: 214 us
  Pallas kernels  201 us (93%)
  local copies, waits for them, and re-layouts  5.28 us (2%)
  other arithmetic  4.66 us (2%)
    pallas_call x1, Pallas kernels, attend(): pl.pallas_call(functools.partial(attend_kernel, chips, heads, group), in_...  112 us
    pallas_call x1, Pallas kernels, project(): pl.pallas_call(functools.partial(project_kernel, chips, parts), out_shape...  88.7 us
  transfers between devices with their start and end apart: 2, of which 1 were waited for; matrix products, arithmetic and copies ran while one was open for 0% of the time, Pallas kernels for 0%

profile of v3, /device:TPU:9, one launch (start us, length us, event | category | flops | bytes accessed | tf_op | source)
XLA Modules:
  0.0 214.3 jit_solution(3619671347920344992)
XLA Ops:
  0.0 1.7 constant_dynamic-slice_fusion.6
  1.7 0.0 copy-start.2
  1.7 0.0 copy-start.3
  1.7 0.0 copy-start.1
  1.7 0.1 pad_maximum_fusion.3
  1.8 0.7 collective-permute-start
  2.6 0.0 copy-done.2
  2.6 0.0 copy-done.3
  2.6 0.5 collective-permute-start.1
  3.1 0.0 copy-done.1
  3.1 0.1 subtract_convert_fusion.1.signs_ref
  3.2 0.1 copy.8.pos_ref
  3.4 1.5 collective-permute-done.1
  4.9 0.1 pad_maximum_fusion.6
  4.9 0.1 broadcast_in_dim.14
  5.0 0.1 mul.91.scale_ref
  5.1 0.1 broadcast_in_dim.6
  5.2 0.1 mul.84
  5.3 0.0 collective-permute-done
  5.3 0.4 broadcast_select_fusion
  5.7 0.6 fusion.1
  6.3 3.7 %fusion.3 = bf16[4096,1,128]{2,0,1:T(8,128)(2,1)S(1)} fusion(bf16[2048,256]{1,0:T(8,128)(2,1)S(1)} %get-tuple-element.7, bf16[2048,256]{1,0:T(8,128)(2,1)S(1)} %get-tuple-element.8, f32[4096]{0:T(1024)S(1)} %mul.84), kind=kLoop, calls=%fused_computation.10 | loop fusion | flops 3145728 | bytes 3162112 | tf_op jit(solution)/shard_map/mul | solution.py:366
  10.0 1.5 pad_bitcast_fusion.vv_ref
  11.6 0.0 copy-start
  11.6 0.2 pad_maximum_fusion.kk_ref
  11.8 0.8 copy-done
  12.6 112.2 %shard_map.73.a_ref = bf16[128,2048]{1,0:T(8,128)(2,1)S(1)} custom-call(bf16[64,4096]{1,0:T(8,128)(2,1)S(1)} %copy-done, bf16[1,256,4096]{2,1,0:T(8,128)(2,1)S(1)} %pad_maximum_fusion.kk_ref, bf16[1,4096,256]{2,1,0:T(8,128)(2,1)} %pad_bitcast_fusion.vv_ref, f32[1,1,4096]{2,1,0:T(1,128)S(1)} %mul.91.scale_ref, s32[512,1]{1,0:T(8,128)S(1)} %copy.8.pos_ref, ...), custom_call_target="tpu_custom_call" | custom-call | flops 25769803776 | bytes 1048576 | tf_op jit(solution)/shard_map/pallas_call | solution.py:174
  124.8 88.7 %shard_map.74 = bf16[128,2048]{1,0:T(8,128)(2,1)S(1)} custom-call(bf16[128,2048]{1,0:T(8,128)(2,1)S(1)} %shard_map.73.a_ref, bf16[4096,2048]{1,0:T(8,128)(2,1)} %w_hbm.1), custom_call_target="tpu_custom_call" | custom-call | flops 8589934592 | bytes 16777216 | tf_op jit(solution)/shard_map/pallas_call | solution.py:306
  213.5 0.8 copy.10
  (7 shorter events, 0.0 us)
Async XLA Ops:
  1.7 0.9 copy-start.2
  1.7 0.9 copy-start.3
  1.7 1.4 copy-start.1
  1.8 3.4 %collective-permute-start = (bf16[2048,256]{1,0:T(8,128)(2,1)S(1)}, bf16[2048,256]{1,0:T(8,128)(2,1)S(1)}, u32[]{:S(2)}, u32[]{:S(2)}) collective-permute-start(bf16[2048,256]{1,0:T(8,128)(2,1)S(1)} %pad_maximum_fusion.3), channel_id=1, source_target_pairs={{0,4},{4,0},{8,12},{12,8},{16,20},{20,16},{24,28},{28,24},{1,5},{5... | collective-permute-start | bytes 3145736 | tf_op jit(solution)/shard_map/ppermute | solution.py:348
  2.6 2.2 %collective-permute-start.1 = (f32[32,2]{0,1:T(2,128)S(1)}, f32[32,2]{0,1:T(2,128)S(1)}, u32[]{:S(2)}, u32[]{:S(2)}) collective-permute-start(f32[32,2]{0,1:T(2,128)S(1)} %pad_maximum_fusion.5), channel_id=1, source_target_pairs={{0,4},{4,0},{8,12},{12,8},{16,20},{20,16},{24,28},{28,24},{1,5},{5... | collective-permute-start | bytes 776 | tf_op jit(solution)/shard_map/ppermute | solution.py:348
  11.6 1.0 copy-start
